TPU v7x, 32 devices: a whole 2x2x4 slice. The times are simulated.
32 devices in a mesh: dp: 2 (over y), ctx: 4 (over z), mp: 4 (over x, core).
Axes of the slice: x: 2, y: 2, z: 4, core: 2. Of those that a mesh axis runs over, the one named last changes fastest.
Arguments:
- tokens_in: bfloat16 [2, 2, 1024, 2048], P(None, 'dp', 'ctx', 'mp'), may hold values from -6 to 6
- out_grad: bfloat16 [2, 2, 1024, 2048], P(None, 'dp', 'ctx', 'mp'), may hold values from -6 to 6
- segment_ids: int32 [2, 2, 1024], P(None, 'dp', 'ctx'), may hold values from 0 to 18, as said below
- w_query: bfloat16 [2048, 2048], P(('dp', 'ctx'), 'mp'), may hold values from -0.1875 to 0.1875
- w_key: bfloat16 [2048, 2048], P(('dp', 'ctx'), 'mp'), may hold values from -0.1875 to 0.1875
- w_value: bfloat16 [2048, 2048], P(('dp', 'ctx'), 'mp'), may hold values from -0.125 to 0.125
- w_out: bfloat16 [2048, 2048], P('mp', ('dp', 'ctx')), may hold values from -0.5 to 0.5
- w_gate: bfloat16 [2048, 8192], P(('dp', 'ctx'), 'mp'), may hold values from -0.125 to 0.125
- w_up: bfloat16 [2048, 8192], P(('dp', 'ctx'), 'mp'), may hold values from -0.125 to 0.125
- w_down: bfloat16 [8192, 2048], P('mp', ('dp', 'ctx')), may hold values from -0.0625 to 0.0625
Outputs:
- tokens_out: bfloat16 [2, 2, 1024, 2048], P(None, 'dp', 'ctx', 'mp')
- grad_in: float32 [2, 2, 1024, 2048], P(None, 'dp', 'ctx', 'mp')
- grad_w_query: float32 [2048, 2048], P(('dp', 'ctx'), 'mp')
- grad_w_key: float32 [2048, 2048], P(('dp', 'ctx'), 'mp')
- grad_w_value: float32 [2048, 2048], P(('dp', 'ctx'), 'mp')
- grad_w_out: float32 [2048, 2048], P('mp', ('dp', 'ctx'))
- grad_w_gate: float32 [2048, 8192], P(('dp', 'ctx'), 'mp')
- grad_w_up: float32 [2048, 8192], P(('dp', 'ctx'), 'mp')
- grad_w_down: float32 [8192, 2048], P('mp', ('dp', 'ctx'))
Inputs may be any that keep to these rules, and one draw needn't show every extreme that they name: `segment_ids`: sequences fall into groups: sequence s of every micro-batch belongs to group s. In each group, one of its 2 sequences over all micro-batches, drawn from the seed, is a single document numbered 1 over all 1024 tokens. Every other sequence holds documents numbered 1, 2, 3 and so on in order, each of 60 to 800 tokens except the last one, which may be cut short, followed by 1 to 128 padding tokens numbered 0. In the first group, the sequence that follows the single-document one (counting micro-batch by micro-batch, cyclically within the group) holds documents of exactly 60 tokens, the last one cut short, and one padding token.
All inputs are finite; a program needn't handle non-finite values.
Results may differ from a plain program's by a relative error of at most 0.018.
Values may be sent and summed in bfloat16 or wider, within the bound.
A program may use at most 256 MiB of HBM per device.

v0:
```python
import math

import jax
import jax.numpy as jnp
from jax import lax
from jax.sharding import PartitionSpec as P

HD = 128


EPSILON = 1e-05
NEG_FILL = -1e30


def layer_norm(values):
    centred = values - jnp.mean(values, axis=-1, keepdims=True)
    inverse = lax.rsqrt(jnp.mean(centred * centred, axis=-1, keepdims=True) + EPSILON)
    return (centred * inverse, inverse)


def norm_backward(upstream, normed, inverse):
    plain_mean = jnp.mean(upstream, axis=-1, keepdims=True)
    cross_mean = jnp.mean(upstream * normed, axis=-1, keepdims=True)
    return inverse * (upstream - plain_mean - normed * cross_mean)


def doc_positions(segment):
    length = segment.shape[-1]
    places = jnp.arange(length, dtype=jnp.int32)
    opening = jnp.ones(segment.shape[:-1] + (1,), dtype=bool)
    change = jnp.concatenate([opening, segment[..., 1:] != segment[..., :-1]], axis=-1)
    starts = lax.cummax(jnp.where(change, places, jnp.int32(0)), axis=segment.ndim - 1)
    return places - starts


def rope_angles(positions):
    freq_table = jnp.power(10000.0, -2.0 * jnp.arange(HD // 2, dtype=jnp.float32) / HD)
    turned = positions.astype(jnp.float32)[..., None] * freq_table
    return (jnp.cos(turned), jnp.sin(turned))


def rope_turn(values, cosine, sine_part):
    half_size = values.shape[-1] // 2
    leading = values[..., :half_size]
    trailing = values[..., half_size:]
    return jnp.concatenate(
        [leading * cosine - trailing * sine_part, trailing * cosine + leading * sine_part], axis=-1
    )


def dot_rows(left_mat, right_mat):
    return lax.dot_general(
        left_mat, right_mat, (((1,), (1,)), ((), ())), preferred_element_type=jnp.float32
    )


def dot_cols(left_mat, right_mat):
    return lax.dot_general(
        left_mat, right_mat, (((0,), (0,)), ((), ())), preferred_element_type=jnp.float32
    )


def fetch_weights(w_query, w_key, w_value, w_gate, w_up, w_out, w_down):
    return (
        lax.all_gather(w_query, ("dp", "ctx"), axis=0, tiled=True),
        lax.all_gather(w_key, ("dp", "ctx"), axis=0, tiled=True),
        lax.all_gather(w_value, ("dp", "ctx"), axis=0, tiled=True),
        lax.all_gather(w_gate, ("dp", "ctx"), axis=0, tiled=True),
        lax.all_gather(w_up, ("dp", "ctx"), axis=0, tiled=True),
        lax.all_gather(w_out, ("dp", "ctx"), axis=1, tiled=True),
        lax.all_gather(w_down, ("dp", "ctx"), axis=1, tiled=True),
    )


def per_device(
    tokens_in, out_grad, segment_ids, w_query, w_key, w_value, w_out, w_gate, w_up, w_down
):
    micro_count = tokens_in.shape[0]
    seq_local = tokens_in.shape[1]
    span_len = tokens_in.shape[2]
    local_width = tokens_in.shape[3]
    ctx_index = lax.axis_index("ctx")
    model_index = lax.axis_index("mp")
    tokens_all, grads_all = (
        lax.all_gather(tokens_in, "mp", axis=3, tiled=True),
        lax.all_gather(out_grad, "mp", axis=3, tiled=True),
    )
    segments_all = lax.all_gather(segment_ids, "ctx", axis=2, tiled=True)
    feature_width = tokens_all.shape[3]
    seq_length = segments_all.shape[2]
    row_count = seq_local * span_len
    score_scale = 1.0 / math.sqrt(HD)
    positions = doc_positions(segments_all)
    query_places = ctx_index * span_len + jnp.arange(span_len, dtype=jnp.int32)
    key_places = jnp.arange(seq_length, dtype=jnp.int32)
    causal = key_places[None, :] <= query_places[:, None]
    outputs = []
    input_grads = []
    totals = None
    for micro_step in range(micro_count):
        full_weights = fetch_weights(w_query, w_key, w_value, w_gate, w_up, w_out, w_down)
        query_full, key_full, value_full, gate_full, up_full, out_full, down_full = full_weights
        head_count = query_full.shape[1] // HD
        segment_seq = segments_all[micro_step]
        segment_own = lax.dynamic_slice_in_dim(segment_seq, ctx_index * span_len, span_len, 1)
        position_own = lax.dynamic_slice_in_dim(
            positions[micro_step], ctx_index * span_len, span_len, 1
        )
        allowed = (segment_own[:, :, None] == segment_seq[:, None, :]) & causal[None]
        cosine, sine_part = rope_angles(position_own)
        cosine = cosine[:, :, None, :]
        sine_part = sine_part[:, :, None, :]
        inputs = tokens_all[micro_step].astype(jnp.float32)
        normed, inverse_one = layer_norm(inputs)
        normed_low = normed.astype(jnp.bfloat16).reshape(row_count, feature_width)

        def project(matrix):
            product = jnp.dot(normed_low, matrix, preferred_element_type=jnp.float32)
            return product.reshape(seq_local, span_len, head_count, HD)

        query_low = (
            rope_turn(project(query_full), cosine, sine_part)
            .astype(jnp.bfloat16)
            .reshape(seq_local, span_len, head_count * HD)
        )
        key_low = (
            rope_turn(project(key_full), cosine, sine_part)
            .astype(jnp.bfloat16)
            .reshape(seq_local, span_len, head_count * HD)
        )
        value_low = (
            project(value_full).astype(jnp.bfloat16).reshape(seq_local, span_len, head_count * HD)
        )
        key_seq, value_seq = (
            lax.all_gather(key_low, "ctx", axis=1, tiled=True),
            lax.all_gather(value_low, "ctx", axis=1, tiled=True),
        )
        mixed_parts = []
        log_totals = []
        for head_index in range(head_count):
            head_cols = slice(head_index * HD, (head_index + 1) * HD)
            scores = (
                jnp.einsum(
                    "sqd,skd->sqk",
                    query_low[..., head_cols],
                    key_seq[..., head_cols],
                    preferred_element_type=jnp.float32,
                )
                * score_scale
            )
            scores = jnp.where(allowed, scores, NEG_FILL)
            highest = jnp.max(scores, axis=-1, keepdims=True)
            exp_terms = jnp.exp(scores - highest)
            total_exp = jnp.sum(exp_terms, axis=-1, keepdims=True)
            probs_low = (exp_terms / total_exp).astype(jnp.bfloat16)
            mixed_parts.append(
                jnp.einsum(
                    "sqk,skd->sqd",
                    probs_low,
                    value_seq[..., head_cols],
                    preferred_element_type=jnp.float32,
                )
            )
            log_totals.append(highest + jnp.log(total_exp))
        mixed_low = (
            jnp.concatenate(mixed_parts, axis=-1)
            .astype(jnp.bfloat16)
            .reshape(row_count, head_count * HD)
        )
        branch = jnp.dot(mixed_low, out_full, preferred_element_type=jnp.float32)
        branch = lax.psum(branch, "mp")
        residual = inputs + branch.reshape(seq_local, span_len, feature_width)
        normed_two, inverse_two = layer_norm(residual)
        second_low = normed_two.astype(jnp.bfloat16).reshape(row_count, feature_width)
        gate_lin = jnp.dot(second_low, gate_full, preferred_element_type=jnp.float32)
        up_lin = jnp.dot(second_low, up_full, preferred_element_type=jnp.float32)
        sigmoid_gate = jax.nn.sigmoid(gate_lin)
        hidden_low = (gate_lin * sigmoid_gate * up_lin).astype(jnp.bfloat16)
        feed_terms = jnp.dot(hidden_low, down_full, preferred_element_type=jnp.float32).reshape(
            seq_local, span_len, feature_width
        )
        feed_own = lax.psum_scatter(
            feed_terms.astype(jnp.bfloat16), "mp", scatter_dimension=2, tiled=True
        ).astype(jnp.float32)
        residual_own = lax.dynamic_slice_in_dim(residual, model_index * local_width, local_width, 2)
        outputs.append((residual_own + feed_own).astype(jnp.bfloat16))
        back_weights = (
            lax.all_gather(w_query, ("dp", "ctx"), axis=0, tiled=True),
            lax.all_gather(w_key, ("dp", "ctx"), axis=0, tiled=True),
            lax.all_gather(w_value, ("dp", "ctx"), axis=0, tiled=True),
            lax.all_gather(w_gate, ("dp", "ctx"), axis=0, tiled=True),
            lax.all_gather(w_up, ("dp", "ctx"), axis=0, tiled=True),
            lax.all_gather(w_out, ("dp", "ctx"), axis=1, tiled=True),
            lax.all_gather(w_down, ("dp", "ctx"), axis=1, tiled=True),
        )
        key_back, value_back = (
            lax.all_gather(key_low, "ctx", axis=1, tiled=True),
            lax.all_gather(value_low, "ctx", axis=1, tiled=True),
        )
        query_back, key_mat, value_mat, gate_back, up_back, out_back, down_back = back_weights
        grad_low = grads_all[micro_step].reshape(row_count, feature_width)
        grad_float = grads_all[micro_step].astype(jnp.float32)
        hidden_grad = dot_rows(grad_low, down_back)
        gate_grad = (
            hidden_grad * up_lin * sigmoid_gate * (1.0 + gate_lin * (1.0 - sigmoid_gate))
        ).astype(jnp.bfloat16)
        up_grad = (hidden_grad * gate_lin * sigmoid_gate).astype(jnp.bfloat16)
        normed_grad = dot_rows(gate_grad, gate_back) + dot_rows(up_grad, up_back)
        normed_grad = lax.psum(normed_grad, "mp").reshape(seq_local, span_len, feature_width)
        residual_grad = grad_float + norm_backward(normed_grad, normed_two, inverse_two)
        residual_low = residual_grad.astype(jnp.bfloat16).reshape(row_count, feature_width)
        mixed_grad = (
            dot_rows(residual_low, out_back)
            .astype(jnp.bfloat16)
            .reshape(seq_local, span_len, head_count * HD)
        )
        query_parts = []
        key_parts = []
        value_parts = []
        for head_index in range(head_count):
            head_cols = slice(head_index * HD, (head_index + 1) * HD)
            query_head = query_low[..., head_cols]
            key_head = key_back[..., head_cols]
            mixed_head = mixed_grad[..., head_cols]
            scores = (
                jnp.einsum("sqd,skd->sqk", query_head, key_head, preferred_element_type=jnp.float32)
                * score_scale
            )
            scores = jnp.where(allowed, scores, NEG_FILL)
            probs = jnp.exp(scores - log_totals[head_index])
            probs_low = probs.astype(jnp.bfloat16)
            value_parts.append(
                jnp.einsum(
                    "sqk,sqd->skd", probs_low, mixed_head, preferred_element_type=jnp.float32
                )
            )
            probs_grad = jnp.einsum(
                "sqd,skd->sqk",
                mixed_head,
                value_back[..., head_cols],
                preferred_element_type=jnp.float32,
            )
            row_dot = jnp.sum(probs * probs_grad, axis=-1, keepdims=True)
            scores_grad = (probs * (probs_grad - row_dot)).astype(jnp.bfloat16)
            query_parts.append(
                jnp.einsum(
                    "sqk,skd->sqd", scores_grad, key_head, preferred_element_type=jnp.float32
                )
                * score_scale
            )
            key_parts.append(
                jnp.einsum(
                    "sqk,sqd->skd", scores_grad, query_head, preferred_element_type=jnp.float32
                )
                * score_scale
            )
        key_terms = jnp.concatenate(key_parts, axis=-1)
        value_terms = jnp.concatenate(value_parts, axis=-1)
        key_grad_own, value_grad_own = (
            lax.psum_scatter(key_terms, "ctx", scatter_dimension=1, tiled=True),
            lax.psum_scatter(value_terms, "ctx", scatter_dimension=1, tiled=True),
        )
        query_sum = jnp.concatenate(query_parts, axis=-1).reshape(
            seq_local, span_len, head_count, HD
        )
        query_grad = (
            rope_turn(query_sum, cosine, -sine_part)
            .astype(jnp.bfloat16)
            .reshape(row_count, head_count * HD)
        )
        key_grad = (
            rope_turn(key_grad_own.reshape(seq_local, span_len, head_count, HD), cosine, -sine_part)
            .astype(jnp.bfloat16)
            .reshape(row_count, head_count * HD)
        )
        value_grad = value_grad_own.astype(jnp.bfloat16).reshape(row_count, head_count * HD)
        input_terms = (
            dot_rows(query_grad, query_back)
            + dot_rows(key_grad, key_mat)
            + dot_rows(value_grad, value_mat)
        )
        input_sum = (
            lax.psum(input_terms.astype(jnp.bfloat16), "mp")
            .astype(jnp.float32)
            .reshape(seq_local, span_len, feature_width)
        )
        grad_whole = residual_grad + norm_backward(input_sum, normed, inverse_one)
        input_grads.append(
            lax.dynamic_slice_in_dim(grad_whole, model_index * local_width, local_width, 2)
        )
        new_terms = (
            dot_cols(normed_low, query_grad),
            dot_cols(normed_low, key_grad),
            dot_cols(normed_low, value_grad),
            dot_cols(second_low, gate_grad),
            dot_cols(second_low, up_grad),
            dot_cols(mixed_low, residual_low),
            dot_cols(hidden_low, grad_low),
        )
        if totals is None:
            totals = new_terms
        else:
            totals = tuple((older + newer for older, newer in zip(totals, new_terms)))
    grads_total = (
        lax.psum_scatter(
            totals[0].astype(jnp.bfloat16), ("dp", "ctx"), scatter_dimension=0, tiled=True
        ).astype(jnp.float32),
        lax.psum_scatter(
            totals[1].astype(jnp.bfloat16), ("dp", "ctx"), scatter_dimension=0, tiled=True
        ).astype(jnp.float32),
        lax.psum_scatter(
            totals[2].astype(jnp.bfloat16), ("dp", "ctx"), scatter_dimension=0, tiled=True
        ).astype(jnp.float32),
        lax.psum_scatter(
            totals[3].astype(jnp.bfloat16), ("dp", "ctx"), scatter_dimension=0, tiled=True
        ).astype(jnp.float32),
        lax.psum_scatter(
            totals[4].astype(jnp.bfloat16), ("dp", "ctx"), scatter_dimension=0, tiled=True
        ).astype(jnp.float32),
        lax.psum_scatter(
            totals[5].astype(jnp.bfloat16), ("dp", "ctx"), scatter_dimension=1, tiled=True
        ).astype(jnp.float32),
        lax.psum_scatter(
            totals[6].astype(jnp.bfloat16), ("dp", "ctx"), scatter_dimension=1, tiled=True
        ).astype(jnp.float32),
    )
    return (
        jnp.stack(outputs, axis=0),
        jnp.stack(input_grads, axis=0),
        grads_total[0],
        grads_total[1],
        grads_total[2],
        grads_total[5],
        grads_total[3],
        grads_total[4],
        grads_total[6],
    )


def solution(mesh):
    in_specs = (
        P(None, "dp", "ctx", "mp"),
        P(None, "dp", "ctx", "mp"),
        P(None, "dp", "ctx"),
        P(("dp", "ctx"), "mp"),
        P(("dp", "ctx"), "mp"),
        P(("dp", "ctx"), "mp"),
        P("mp", ("dp", "ctx")),
        P(("dp", "ctx"), "mp"),
        P(("dp", "ctx"), "mp"),
        P("mp", ("dp", "ctx")),
    )
    out_specs = (
        P(None, "dp", "ctx", "mp"),
        P(None, "dp", "ctx", "mp"),
        P(("dp", "ctx"), "mp"),
        P(("dp", "ctx"), "mp"),
        P(("dp", "ctx"), "mp"),
        P("mp", ("dp", "ctx")),
        P(("dp", "ctx"), "mp"),
        P(("dp", "ctx"), "mp"),
        P("mp", ("dp", "ctx")),
    )
    return jax.shard_map(
        per_device, mesh=mesh, in_specs=in_specs, out_specs=out_specs, check_vma=False
    )
```

profile of v0, /device:TPU:0, one launch (start us, length us, event | category | flops | bytes accessed | tf_op | source)
XLA Modules:
  0.0 2036.8 jit_solution(12763182694997986265)
XLA Ops:
  37.8 48.6 %all-gather.16.cloned.1.call-done = bf16[2048,512]{1,0:T(8,128)(2,1)} async-done(((bf16[256,512]{1,0:T(8,128)(2,1)}), bf16[2048,512]{1,0:T(8,128)(2,1)}) %all-gather.16.cloned.1.call-update) | async-done | bytes 2097168 | tf_op jit(solution)/shard_map/all_gather | solution.py:65
  90.3 46.0 %all-gather.18.cloned.1.call-done = bf16[2048,512]{1,0:T(8,128)(2,1)} async-done(((bf16[256,512]{1,0:T(8,128)(2,1)}), bf16[2048,512]{1,0:T(8,128)(2,1)}) %all-gather.18.cloned.1.call-update) | async-done | bytes 2097168 | tf_op jit(solution)/shard_map/all_gather | solution.py:66
  149.1 37.0 %all-gather.22.cloned.1.call-done = bf16[2048,512]{1,0:T(8,128)(2,1)} async-done(((bf16[256,512]{1,0:T(8,128)(2,1)}), bf16[2048,512]{1,0:T(8,128)(2,1)}) %all-gather.22.cloned.1.call-update) | async-done | bytes 2097168 | tf_op jit(solution)/shard_map/all_gather | solution.py:67
  197.6 19.2 all-gather.34.cloned.1.call-done
  223.0 24.3 %all-gather.20.cloned.1.call-done = bf16[1,1024,512]{1,2,0:T(8,128)(2,1)} async-done(((bf16[1,256,512]{1,2,0:T(8,128)(2,1)}), bf16[1,1024,512]{1,2,0:T(8,128)(2,1)}) %all-gather.20.cloned.1.call-update) | async-done | bytes 1048592 | tf_op jit(solution)/shard_map/all_gather | solution.py:135
  255.6 22.4 %all-gather.36.cloned.1.call-done = bf16[1,1024,512]{1,2,0:T(8,128)(2,1)} async-done(((bf16[1,256,512]{1,2,0:T(8,128)(2,1)}), bf16[1,1024,512]{1,2,0:T(8,128)(2,1)}) %all-gather.36.cloned.1.call-update) | async-done | bytes 1048592 | tf_op jit(solution)/shard_map/all_gather | solution.py:136
  282.8 25.8 %all-gather.24.cloned.1.call-done = bf16[1,1024,512]{1,2,0:T(8,128)(2,1)} async-done(((bf16[1,256,512]{1,2,0:T(8,128)(2,1)}), bf16[1,1024,512]{1,2,0:T(8,128)(2,1)}) %all-gather.24.cloned.1.call-update) | async-done | bytes 1048592 | tf_op jit(solution)/shard_map/all_gather | solution.py:136
  313.8 46.3 %all-gather.26.cloned.1.call-done = bf16[512,2048]{1,0:T(8,128)(2,1)} async-done(((bf16[512,256]{1,0:T(8,128)(2,1)}), bf16[512,2048]{1,0:T(8,128)(2,1)}) %all-gather.26.cloned.1.call-update) | async-done | bytes 2097168 | tf_op jit(solution)/shard_map/all_gather | solution.py:70
  369.1 80.9 %all-reduce.10.cloned.1.call-done = (f32[256,2048]{1,0:T(8,128)}, f32[256,2048]{1,0:T(8,128)}) async-done(((f32[256,2048]{1,0:T(8,128)}, f32[256,2048]{1,0:T(8,128)}), (f32[256,2048]{1,0:T(8,128)}, f32[256,2048]{1,0:T(8,128)})) %all-reduce.10.cloned.1.call-update) | async-done | bytes 4194320 | tf_op jit(solution)/shard_map/psum | solution.py:171
  456.6 120.9 %all-gather.28.cloned.1.call-done = bf16[2048,2048]{1,0:T(8,128)(2,1)} async-done(((bf16[256,2048]{1,0:T(8,128)(2,1)}), bf16[2048,2048]{1,0:T(8,128)(2,1)}) %all-gather.28.cloned.1.call-update) | async-done | bytes 8388624 | tf_op jit(solution)/shard_map/all_gather | solution.py:68
  584.8 118.0 %all-gather.30.cloned.1.call-done = bf16[2048,2048]{1,0:T(8,128)(2,1)} async-done(((bf16[256,2048]{1,0:T(8,128)(2,1)}), bf16[2048,2048]{1,0:T(8,128)(2,1)}) %all-gather.30.cloned.1.call-update) | async-done | bytes 8388624 | tf_op jit(solution)/shard_map/all_gather | solution.py:69
  725.3 127.5 %all-gather.32.cloned.1.call-done = bf16[2048,2048]{1,0:T(8,128)(2,1)} async-done(((bf16[2048,256]{1,0:T(8,128)(2,1)}), bf16[2048,2048]{1,0:T(8,128)(2,1)}) %all-gather.32.cloned.1.call-update) | async-done | bytes 8388624 | tf_op jit(solution)/shard_map/all_gather | solution.py:71
  894.0 83.3 %all-reduce.8.cloned.1.call-done = (f32[256,2048]{1,0:T(8,128)}, f32[256,2048]{1,0:T(8,128)}) async-done(((f32[256,2048]{1,0:T(8,128)}, f32[256,2048]{1,0:T(8,128)}), (f32[256,2048]{1,0:T(8,128)}, f32[256,2048]{1,0:T(8,128)})) %all-reduce.8.cloned.1.call-update) | async-done | bytes 4194320 | tf_op jit(solution)/shard_map/psum | solution.py:209
  1049.6 37.5 %reduce-scatter.18.cloned.1.call-done = f32[1,256,512]{1,2,0:T(8,128)} async-done(((f32[1,1024,512]{1,2,0:T(8,128)}), f32[1,256,512]{1,2,0:T(8,128)}) %reduce-scatter.18.cloned.1.call-update) | async-done | bytes 524304 | tf_op jit(solution)/shard_map/reduce_scatter | solution.py:260
  1093.8 38.6 %reduce-scatter.24.cloned.1.call-done = f32[1,256,512]{1,2,0:T(8,128)} async-done(((f32[1,1024,512]{1,2,0:T(8,128)}), f32[1,256,512]{1,2,0:T(8,128)}) %reduce-scatter.24.cloned.1.call-update) | async-done | bytes 524304 | tf_op jit(solution)/shard_map/reduce_scatter | solution.py:261
  1138.8 39.2 %reduce-scatter.20.cloned.1.call-done = f32[1,256,512]{1,2,0:T(8,128)} async-done(((f32[1,1024,512]{1,2,0:T(8,128)}), f32[1,256,512]{1,2,0:T(8,128)}) %reduce-scatter.20.cloned.1.call-update) | async-done | bytes 524304 | tf_op jit(solution)/shard_map/reduce_scatter | solution.py:261
  1262.9 41.8 %reduce-scatter.32.cloned.1.call-done = bf16[512,256]{1,0:T(8,128)(2,1)} async-done(((bf16[512,2048]{1,0:T(8,128)(2,1)}), bf16[512,256]{1,0:T(8,128)(2,1)}) %reduce-scatter.32.cloned.1.call-update) | async-done | bytes 262160 | tf_op jit(solution)/shard_map/reduce_scatter | solution.py:320
  1306.5 51.3 %all-reduce.12.cloned.1.call-done = (bf16[256,2048]{1,0:T(8,128)(2,1)}, bf16[256,2048]{1,0:T(8,128)(2,1)}) async-done(((bf16[256,2048]{1,0:T(8,128)(2,1)}, bf16[256,2048]{1,0:T(8,128)(2,1)}), (bf16[256,2048]{1,0:T(8,128)(2,1)}, bf16[256,2048]{1,0:T(8,128)(2,1)})) %all-reduce.12.cloned.1.call-update) | async-done | bytes 2097168 | tf_op jit(solution)/shard_map/psum | solution.py:283
  1365.6 63.7 %reduce-scatter.26.cloned.1.call-done = bf16[256,512]{1,0:T(8,128)(2,1)} async-done(((bf16[2048,512]{1,0:T(8,128)(2,1)}), bf16[256,512]{1,0:T(8,128)(2,1)}) %reduce-scatter.26.cloned.1.call-update) | async-done | bytes 262160 | tf_op jit(solution)/shard_map/reduce_scatter | solution.py:305
  1431.2 69.0 %reduce-scatter.28.cloned.1.call-done = bf16[256,512]{1,0:T(8,128)(2,1)} async-done(((bf16[2048,512]{1,0:T(8,128)(2,1)}), bf16[256,512]{1,0:T(8,128)(2,1)}) %reduce-scatter.28.cloned.1.call-update) | async-done | bytes 262160 | tf_op jit(solution)/shard_map/reduce_scatter | solution.py:308
  1501.9 69.0 %reduce-scatter.30.cloned.1.call-done = bf16[256,512]{1,0:T(8,128)(2,1)} async-done(((bf16[2048,512]{1,0:T(8,128)(2,1)}), bf16[256,512]{1,0:T(8,128)(2,1)}) %reduce-scatter.30.cloned.1.call-update) | async-done | bytes 262160 | tf_op jit(solution)/shard_map/reduce_scatter | solution.py:311
  1572.7 150.2 %reduce-scatter.34.cloned.1.call-done = bf16[256,2048]{1,0:T(8,128)(2,1)} async-done(((bf16[2048,2048]{1,0:T(8,128)(2,1)}), bf16[256,2048]{1,0:T(8,128)(2,1)}) %reduce-scatter.34.cloned.1.call-update) | async-done | bytes 1048592 | tf_op jit(solution)/shard_map/reduce_scatter | solution.py:314
  1725.6 148.9 %reduce-scatter.36.cloned.1.call-done = bf16[256,2048]{1,0:T(8,128)(2,1)} async-done(((bf16[2048,2048]{1,0:T(8,128)(2,1)}), bf16[256,2048]{1,0:T(8,128)(2,1)}) %reduce-scatter.36.cloned.1.call-update) | async-done | bytes 1048592 | tf_op jit(solution)/shard_map/reduce_scatter | solution.py:317
  1877.3 149.8 %reduce-scatter.38.cloned.1.call-done = bf16[2048,256]{1,0:T(8,128)(2,1)} async-done(((bf16[2048,2048]{1,0:T(8,128)(2,1)}), bf16[2048,256]{1,0:T(8,128)(2,1)}) %reduce-scatter.38.cloned.1.call-update) | async-done | bytes 1048592 | tf_op jit(solution)/shard_map/reduce_scatter | solution.py:323
  (578 shorter events, 360.9 us)
Async XLA Ops:
  8.7 127.7 %all-gather.18.cloned.1.call-start = ((), (), s32[]{:S(2)}) async-start(), calls=%async_computation.15 | async-start | bytes 2359296 | tf_op jit(solution)/shard_map/all_gather | solution.py:66
  9.4 176.7 %all-gather.22.cloned.1.call-start = ((), (), s32[]{:S(2)}) async-start(), calls=%async_computation.17 | async-start | bytes 2359296 | tf_op jit(solution)/shard_map/all_gather | solution.py:67
  10.0 206.8 %all-gather.34.cloned.1.call-start = ((), (), s32[]{:S(2)}) async-start(), calls=%async_computation.24 | async-start | bytes 1310720 | tf_op jit(solution)/shard_map/all_gather | solution.py:135
  149.0 128.9 %all-gather.36.cloned.1.call-start = ((), (), s32[]{:S(2)}) async-start(), calls=%async_computation.25 | async-start | bytes 1310720 | tf_op jit(solution)/shard_map/all_gather | solution.py:136
  196.5 163.6 %all-gather.26.cloned.1.call-start = ((), (), s32[]{:S(2)}) async-start(), calls=%async_computation.19 | async-start | bytes 2359296 | tf_op jit(solution)/shard_map/all_gather | solution.py:70
  197.2 252.8 %all-reduce.10.cloned.1.call-start = ((), (), s32[]{:S(2)}) async-start(), calls=%async_computation.40 | async-start | bytes 8388608 | tf_op jit(solution)/shard_map/psum | solution.py:171
  366.0 211.5 %all-gather.28.cloned.1.call-start = ((), (), s32[]{:S(2)}) async-start(), calls=%async_computation.20 | async-start | bytes 9437184 | tf_op jit(solution)/shard_map/all_gather | solution.py:68
  366.7 336.1 %all-gather.30.cloned.1.call-start = ((), (), s32[]{:S(2)}) async-start(), calls=%async_computation.21 | async-start | bytes 9437184 | tf_op jit(solution)/shard_map/all_gather | solution.py:69
  367.3 357.9 %all-gather.38.cloned.1.call-start = ((), (), s32[]{:S(2)}) async-start(), calls=%async_computation.27 | async-start | bytes 2621440 | tf_op jit(solution)/shard_map/all_gather | solution.py:86
  368.1 484.7 %all-gather.32.cloned.1.call-start = ((), (), s32[]{:S(2)}) async-start(), calls=%async_computation.22 | async-start | bytes 9437184 | tf_op jit(solution)/shard_map/all_gather | solution.py:71
  368.6 608.7 %all-reduce.8.cloned.1.call-start = ((), (), s32[]{:S(2)}) async-start(), calls=%async_computation.39 | async-start | bytes 8388608 | tf_op jit(solution)/shard_map/psum | solution.py:209
  893.3 155.0 %reduce-scatter.22.cloned.1.call-start = ((), (), s32[]{:S(2)}) async-start(), calls=%async_computation.30 | async-start | bytes 2621440 | tf_op jit(solution)/shard_map/reduce_scatter | solution.py:260
  1011.7 120.7 %reduce-scatter.24.cloned.1.call-start = ((), (), s32[]{:S(2)}) async-start(), calls=%async_computation.31 | async-start | bytes 2621440 | tf_op jit(solution)/shard_map/reduce_scatter | solution.py:261
  1016.4 161.7 %reduce-scatter.20.cloned.1.call-start = ((), (), s32[]{:S(2)}) async-start(), calls=%async_computation.29 | async-start | bytes 2621440 | tf_op jit(solution)/shard_map/reduce_scatter | solution.py:261
  1021.3 238.3 %reduce-scatter.16.cloned.1.call-start = ((), (), s32[]{:S(2)}) async-start(), calls=%async_computation.26 | async-start | bytes 1310720 | tf_op jit(solution)/shard_map/reduce_scatter | solution.py:182
  1028.6 232.3 %reduce-scatter.14.cloned.1.call-start = ((), (), s32[]{:S(2)}) async-start(), calls=%async_computation.23 | async-start | bytes 1310720 | tf_op jit(solution)/shard_map/reduce_scatter | solution.py:182
  1035.5 269.3 %reduce-scatter.32.cloned.1.call-start = ((), (), s32[]{:S(2)}) async-start(), calls=%async_computation.35 | async-start | bytes 2359296 | tf_op jit(solution)/shard_map/reduce_scatter | solution.py:320
  1040.2 317.6 %all-reduce.12.cloned.1.call-start = ((), (), s32[]{:S(2)}) async-start(), calls=%async_computation.41 | async-start | bytes 4194304 | tf_op jit(solution)/shard_map/psum | solution.py:283
  1182.2 247.1 %reduce-scatter.26.cloned.1.call-start = ((), (), s32[]{:S(2)}) async-start(), calls=%async_computation.32 | async-start | bytes 2359296 | tf_op jit(solution)/shard_map/reduce_scatter | solution.py:305
  1186.0 314.1 %reduce-scatter.28.cloned.1.call-start = ((), (), s32[]{:S(2)}) async-start(), calls=%async_computation.33 | async-start | bytes 2359296 | tf_op jit(solution)/shard_map/reduce_scatter | solution.py:308
  1189.3 381.6 %reduce-scatter.30.cloned.1.call-start = ((), (), s32[]{:S(2)}) async-start(), calls=%async_computation.34 | async-start | bytes 2359296 | tf_op jit(solution)/shard_map/reduce_scatter | solution.py:311
  1193.5 529.4 %reduce-scatter.34.cloned.1.call-start = ((), (), s32[]{:S(2)}) async-start(), calls=%async_computation.36 | async-start | bytes 9437184 | tf_op jit(solution)/shard_map/reduce_scatter | solution.py:314
  1215.9 658.7 %reduce-scatter.36.cloned.1.call-start = ((), (), s32[]{:S(2)}) async-start(), calls=%async_computation.37 | async-start | bytes 9437184 | tf_op jit(solution)/shard_map/reduce_scatter | solution.py:317
  1237.1 790.0 %reduce-scatter.38.cloned.1.call-start = ((), (), s32[]{:S(2)}) async-start(), calls=%async_computation.38 | async-start | bytes 9437184 | tf_op jit(solution)/shard_map/reduce_scatter | solution.py:323
  (164 other events, 2466.4 us)
Sparse Core Ops, SparseCore 0:
  37.0 49.3 all-gather.15
  88.5 47.7 all-gather.17
  138.3 47.7 all-gather.21
  188.1 28.6 all-gather.33
  218.8 28.4 all-gather.19
  280.1 28.4 all-gather.23
  310.6 49.3 all-gather.25
  366.1 83.8 all-reduce.9
  452.4 125.0 all-gather.27
  579.7 123.1 all-gather.29
  727.3 125.4 all-gather.31
  893.4 83.8 all-reduce.7
  997.6 43.9 reduce-scatter.21
  1043.8 43.3 reduce-scatter.17
  1089.3 43.1 reduce-scatter.23
  1134.8 43.1 reduce-scatter.19
  1236.4 68.2 reduce-scatter.31
  1307.2 50.5 all-reduce.11
  1361.6 67.6 reduce-scatter.25
  1433.3 66.8 reduce-scatter.27
  1503.9 66.9 reduce-scatter.29
  1574.8 148.0 reduce-scatter.33
  1726.5 148.0 reduce-scatter.35
  1878.6 148.4 reduce-scatter.37
  (5 shorter events, 123.3 us)
where the time goes:
time: 2040 us
  waiting for transfers between devices  1680 us (82%)
  matrix products  222 us (11%)
  other arithmetic  64.6 us (3%)
  local copies, waits for them, and re-layouts  35.3 us (2%)
    reduce_scatter x1, waiting for transfers between devices, per_device(): lax.psum_scatter(totals[3].astype(jnp.bfloat16), ('dp', 'ctx'), scatter_d...  150 us
    reduce_scatter x1, waiting for transfers between devices, per_device(): lax.psum_scatter(totals[6].astype(jnp.bfloat16), ('dp', 'ctx'), scatter_d...  150 us
    reduce_scatter x1, waiting for transfers between devices, per_device(): lax.psum_scatter(totals[4].astype(jnp.bfloat16), ('dp', 'ctx'), scatter_d...  149 us
    all_gather x1, waiting for transfers between devices, fetch_weights(): lax.all_gather(w_down, ('dp', 'ctx'), axis=1, tiled=True)  127 us
    all_gather x1, waiting for transfers between devices, fetch_weights(): lax.all_gather(w_gate, ('dp', 'ctx'), axis=0, tiled=True)  121 us
    all_gather x1, waiting for transfers between devices, fetch_weights(): lax.all_gather(w_up, ('dp', 'ctx'), axis=0, tiled=True)  118 us
    psum x1, waiting for transfers between devices, per_device(): lax.psum(normed_grad, 'mp').reshape(seq_local, span_len, feature_width)  83.3 us
    psum x1, waiting for transfers between devices, per_device(): branch = lax.psum(branch, 'mp')  80.9 us
  transfers between devices with their start and end apart: 29, of which 26 were waited for; matrix products, arithmetic and copies ran while one was open for 12% of the time, Pallas kernels for 0%

commit v1 on v0

--- a/solution.py
+++ b/solution.py
@@ -72,7 +72,7 @@
     )
 
 
-def per_device(
+def per_device_general(
     tokens_in, out_grad, segment_ids, w_query, w_key, w_value, w_out, w_gate, w_up, w_down
 ):
     micro_count = tokens_in.shape[0]
@@ -337,6 +337,240 @@
     )
 
 
+def xor_permute(values, axis, size, mask):
+    return lax.ppermute(values, axis, [(place, place ^ mask) for place in range(size)])
+
+
+def pick_blocks(blocks, index):
+    stack = jnp.stack(blocks, axis=0)
+    return [
+        lax.dynamic_index_in_dim(stack, index ^ place, 0, keepdims=False)
+        for place in range(len(blocks))
+    ]
+
+
+def token_routes(offset):
+    routes = []
+    for high in range(2):
+        for low in range(2):
+            for model in range(4):
+                wanted = model ^ offset
+                routes.append(
+                    ((high * 2 + low) * 4 + model, ((wanted // 2) * 2 + high) * 4 + low * 2 + wanted % 2)
+                )
+    return routes
+
+
+def to_rows(values, model_index, quarter):
+    span_half = values.shape[2] // 2
+    parts = values.reshape(4, span_half, values.shape[3])
+    blocks = []
+    for offset in range(4):
+        part = lax.dynamic_index_in_dim(parts, model_index ^ offset, 0, keepdims=False)
+        blocks.append(lax.ppermute(part, ("ctx", "mp"), token_routes(offset)))
+    return jnp.concatenate(pick_blocks(blocks, quarter), axis=1)
+
+
+def from_rows(rows, model_index, quarter):
+    row_count, width = rows.shape
+    parts = jnp.transpose(rows.reshape(row_count, 4, width // 4), (1, 0, 2))
+    blocks = []
+    for offset in range(4):
+        part = lax.dynamic_index_in_dim(parts, quarter ^ offset, 0, keepdims=False)
+        routes = [(target, source) for source, target in token_routes(offset)]
+        blocks.append(lax.ppermute(part, ("ctx", "mp"), routes))
+    return jnp.concatenate(pick_blocks(blocks, model_index), axis=0).reshape(
+        2, 1, 2 * row_count, width // 4
+    )
+
+
+def half_of(values, axis, which):
+    size = values.shape[axis] // 2
+    return lax.dynamic_slice_in_dim(values, which * size, size, axis)
+
+
+def fetch_stack(shards, axis, low, home):
+    mine = jnp.concatenate([half_of(shard, axis, low) for shard in shards], axis=axis)
+    other = jnp.concatenate([half_of(shard, axis, 1 - low) for shard in shards], axis=axis)
+    near = [
+        mine,
+        xor_permute(other, "ctx", 4, 1),
+        xor_permute(mine, "ctx", 4, 2),
+        xor_permute(other, "ctx", 4, 3),
+    ]
+    far = [xor_permute(block, "dp", 2, 1) for block in near]
+    return jnp.concatenate(pick_blocks(near + far, home), axis=1 - axis)
+
+
+def return_grads(grad, axis, dp_index, high, low):
+    cut = 1 - axis
+    sent = half_of(grad, cut, 1 - dp_index).astype(jnp.bfloat16)
+    total = half_of(grad, cut, dp_index) + xor_permute(sent, "dp", 2, 1).astype(jnp.float32)
+    sent = half_of(total, cut, 1 - high).astype(jnp.bfloat16)
+    total = half_of(total, cut, high) + xor_permute(sent, "ctx", 4, 2).astype(jnp.float32)
+    sent = half_of(total, cut, 1 - low).astype(jnp.bfloat16)
+    mine = half_of(total, cut, low)
+    return mine, xor_permute(sent, "ctx", 4, 1).astype(jnp.float32)
+
+
+def place_halves(mine, other, axis, low):
+    first = jnp.where(low == 0, mine, other)
+    second = jnp.where(low == 0, other, mine)
+    return jnp.concatenate([first, second], axis=axis)
+
+
+GROUPS = [[(high * 2 + low) * 4 + model for low in range(2) for model in range(4)] for high in range(2)]
+
+
+def gather_rows(rows):
+    return lax.all_gather(rows, ("ctx", "mp"), axis=0, tiled=True, axis_index_groups=GROUPS)
+
+
+def scatter_rows(terms):
+    return lax.psum_scatter(
+        terms.astype(jnp.bfloat16),
+        ("ctx", "mp"),
+        scatter_dimension=0,
+        tiled=True,
+        axis_index_groups=GROUPS,
+    ).astype(jnp.float32)
+
+
+def per_device_grouped(
+    tokens_in, out_grad, segment_ids, w_query, w_key, w_value, w_out, w_gate, w_up, w_down
+):
+    dp_index = lax.axis_index("dp")
+    ctx_index = lax.axis_index("ctx")
+    model_index = lax.axis_index("mp")
+    high = ctx_index // 2
+    low = ctx_index % 2
+    quarter = 2 * high + model_index % 2
+    home = dp_index * 4 + ctx_index
+    score_scale = 1.0 / math.sqrt(HD)
+    feature_width = tokens_in.shape[3] * 4
+
+    segments_all = lax.all_gather(segment_ids, "ctx", axis=2, tiled=True)
+    segment = lax.dynamic_index_in_dim(segments_all, high, 0, keepdims=False)[0]
+    length = segment.shape[0]
+    row_count = length // 8
+
+    token_rows = to_rows(tokens_in, model_index, quarter).astype(jnp.float32)
+    query_key_value = fetch_stack((w_query, w_key, w_value), 1, low, home)
+    out_part = fetch_stack((w_out,), 0, low, home)
+    grad_rows = to_rows(out_grad, model_index, quarter)
+    gate_part = fetch_stack((w_gate,), 1, low, home)
+    up_part = fetch_stack((w_up,), 1, low, home)
+    down_part = fetch_stack((w_down,), 0, low, home)
+
+    normed_rows, inverse_one = layer_norm(token_rows)
+    normed_low = gather_rows(normed_rows.astype(jnp.bfloat16))
+
+    places = jnp.arange(length, dtype=jnp.int32)
+    allowed = (segment[:, None] == segment[None, :]) & (places[None, :] <= places[:, None])
+    cosine, sine_part = rope_angles(doc_positions(segment))
+    cosine = cosine[:, None, :]
+    sine_part = sine_part[:, None, :]
+
+    local_cols = query_key_value.shape[1] // 3
+    head_count = local_cols // HD
+    projected = jnp.dot(normed_low, query_key_value, preferred_element_type=jnp.float32)
+
+    def turned(values, sine_used):
+        return (
+            rope_turn(values.reshape(length, head_count, HD), cosine, sine_used)
+            .astype(jnp.bfloat16)
+            .reshape(length, local_cols)
+        )
+
+    query_low = turned(projected[:, :local_cols], sine_part)
+    key_low = turned(projected[:, local_cols : 2 * local_cols], sine_part)
+    value_low = projected[:, 2 * local_cols :].astype(jnp.bfloat16)
+    mixed_parts = []
+    log_totals = []
+    for head_index in range(head_count):
+        cols = slice(head_index * HD, (head_index + 1) * HD)
+        scores = dot_rows(query_low[:, cols], key_low[:, cols]) * score_scale
+        scores = jnp.where(allowed, scores, NEG_FILL)
+        highest = jnp.max(scores, axis=-1, keepdims=True)
+        exp_terms = jnp.exp(scores - highest)
+        total_exp = jnp.sum(exp_terms, axis=-1, keepdims=True)
+        probs_low = (exp_terms / total_exp).astype(jnp.bfloat16)
+        mixed_parts.append(
+            jnp.dot(probs_low, value_low[:, cols], preferred_element_type=jnp.float32)
+        )
+        log_totals.append(highest + jnp.log(total_exp))
+    mixed_low = jnp.concatenate(mixed_parts, axis=-1).astype(jnp.bfloat16)
+    branch = scatter_rows(jnp.dot(mixed_low, out_part, preferred_element_type=jnp.float32))
+    residual = token_rows + branch
+    normed_two, inverse_two = layer_norm(residual)
+    second_low = gather_rows(normed_two.astype(jnp.bfloat16))
+    grad_low = gather_rows(grad_rows)
+    gate_lin = jnp.dot(second_low, gate_part, preferred_element_type=jnp.float32)
+    up_lin = jnp.dot(second_low, up_part, preferred_element_type=jnp.float32)
+    sigmoid_gate = jax.nn.sigmoid(gate_lin)
+    hidden_low = (gate_lin * sigmoid_gate * up_lin).astype(jnp.bfloat16)
+    down_grads = return_grads(dot_cols(hidden_low, grad_low), 0, dp_index, high, low)
+    hidden_grad = dot_rows(grad_low, down_part)
+    gate_grad = (
+        hidden_grad * up_lin * sigmoid_gate * (1.0 + gate_lin * (1.0 - sigmoid_gate))
+    ).astype(jnp.bfloat16)
+    up_grad = (hidden_grad * gate_lin * sigmoid_gate).astype(jnp.bfloat16)
+    normed_grad = scatter_rows(dot_rows(gate_grad, gate_part) + dot_rows(up_grad, up_part))
+    gate_grads = return_grads(dot_cols(second_low, gate_grad), 1, dp_index, high, low)
+    up_grads = return_grads(dot_cols(second_low, up_grad), 1, dp_index, high, low)
+    feed = scatter_rows(jnp.dot(hidden_low, down_part, preferred_element_type=jnp.float32))
+    tokens_out = from_rows((residual + feed).astype(jnp.bfloat16), model_index, quarter)
+    residual_grad = grad_rows.astype(jnp.float32) + norm_backward(
+        normed_grad, normed_two, inverse_two
+    )
+    residual_low = gather_rows(residual_grad.astype(jnp.bfloat16))
+    out_grads = return_grads(dot_cols(mixed_low, residual_low), 0, dp_index, high, low)
+    mixed_grad = dot_rows(residual_low, out_part).astype(jnp.bfloat16)
+    query_parts = []
+    key_parts = []
+    value_parts = []
+    for head_index in range(head_count):
+        cols = slice(head_index * HD, (head_index + 1) * HD)
+        query_head = query_low[:, cols]
+        key_head = key_low[:, cols]
+        mixed_head = mixed_grad[:, cols]
+        scores = dot_rows(query_head, key_head) * score_scale
+        scores = jnp.where(allowed, scores, NEG_FILL)
+        probs = jnp.exp(scores - log_totals[head_index])
+        value_parts.append(dot_cols(probs.astype(jnp.bfloat16), mixed_head))
+        probs_grad = dot_rows(mixed_head, value_low[:, cols])
+        row_dot = jnp.sum(probs * probs_grad, axis=-1, keepdims=True)
+        scores_grad = (probs * (probs_grad - row_dot)).astype(jnp.bfloat16)
+        query_parts.append(
+            jnp.dot(scores_grad, key_head, preferred_element_type=jnp.float32) * score_scale
+        )
+        key_parts.append(dot_cols(scores_grad, query_head) * score_scale)
+    query_grad = turned(jnp.concatenate(query_parts, axis=-1), -sine_part)
+    key_grad = turned(jnp.concatenate(key_parts, axis=-1), -sine_part)
+    value_grad = jnp.concatenate(value_parts, axis=-1).astype(jnp.bfloat16)
+    three_grad = jnp.concatenate([query_grad, key_grad, value_grad], axis=-1)
+    input_sum = scatter_rows(dot_rows(three_grad, query_key_value))
+    three_grads = return_grads(dot_cols(normed_low, three_grad), 1, dp_index, high, low)
+    grad_in_rows = residual_grad + norm_backward(input_sum, normed_rows, inverse_one)
+    grad_in = from_rows(grad_in_rows.astype(jnp.bfloat16), model_index, quarter)
+
+    def columns(pair, which):
+        cols = slice(which * local_cols, (which + 1) * local_cols)
+        return place_halves(pair[0][:, cols], pair[1][:, cols], 1, low)
+
+    return (
+        tokens_out,
+        grad_in.astype(jnp.float32),
+        columns(three_grads, 0),
+        columns(three_grads, 1),
+        columns(three_grads, 2),
+        place_halves(*out_grads, 0, low),
+        place_halves(*gate_grads, 1, low),
+        place_halves(*up_grads, 1, low),
+        place_halves(*down_grads, 0, low),
+    )
+
+
 def solution(mesh):
     in_specs = (
         P(None, "dp", "ctx", "mp"),
@@ -361,6 +595,8 @@
         P(("dp", "ctx"), "mp"),
         P("mp", ("dp", "ctx")),
     )
+    grouped = mesh.shape["ctx"] == 4 and mesh.shape["mp"] == 4 and mesh.shape["dp"] == 2
+    per_device = per_device_grouped if grouped else per_device_general
     return jax.shard_map(
         per_device, mesh=mesh, in_specs=in_specs, out_specs=out_specs, check_vma=False
     )

time: 2040 us -> 986 us (0.48)
  waiting for transfers between devices: 1680 us -> 581 us
  matrix products: 222 us -> 109 us
  starting transfers between devices: 2.83 us -> 99.8 us
  local copies, waits for them, and re-layouts: 35.3 us -> 75.5 us
  blocking collectives: 12.9 us -> 34.3 us
    reduce_scatter x13 -> x4, waiting for transfers between devices: 808 us -> 137 us  [scatter_rows(): lax.psum_scatter(terms.astype(jnp.bfloat16), ('ctx', 'mp'), scatter_dimen...]
    all_gather x13 -> x4, waiting for transfers between devices: 653 us -> 0.03 us  [gather_rows(): lax.all_gather(rows, ('ctx', 'mp'), axis=0, tiled=True, axis_index_groups...]
    ppermute x0 -> x66, waiting for transfers between devices: none -> 444 us  [the longest x50 438 us: xor_permute(): lax.ppermute(values, axis, [(place, place ^ mask) for place in range(size)])]
    psum x3 -> x0, waiting for transfers between devices: 216 us -> none  [the longest x1 83.3 us: per_device(): lax.psum(normed_grad, 'mp').reshape(seq_local, span_len, feature_width)]
    ppermute x0 -> x66, starting transfers between devices: none -> 99.5 us  [the longest x50 72.4 us: xor_permute(): lax.ppermute(values, axis, [(place, place ^ mask) for place in range(size)])]
    dot_general x14 -> x9, matrix products: 77.5 us -> 25.6 us  [dot_cols(): lax.dot_general(left_mat, right_mat, (((0,), (0,)), ((), ())), preferred_...]
    dot_general x62 -> x9, matrix products: 86.4 us -> 38 us  [the longest x1 10.1 us: per_device_grouped(): up_lin = jnp.dot(second_low, up_part, preferred_element_type=jnp.float32)]
    unnamed x318 -> x224, local copies, waits for them, and re-layouts: 23.3 us -> 54.9 us
  transfers between devices with their start and end apart: 29 -> 74, of which waited for: 26 -> 33; matrix products, arithmetic and copies ran while one was open for 12% -> 17% of each run, Pallas kernels for 0% -> 0%
where the time goes in v1:
time: 986 us; the launch traced here: 972 us
  waiting for transfers between devices  581 us (59%)
  matrix products  109 us (11%)
  starting transfers between devices  99.8 us (10%)
  local copies, waits for them, and re-layouts  75.5 us (8%)
  other arithmetic  55.6 us (6%)
  blocking collectives  34.3 us (3%)
  between operations  16.2 us (2%)
    ppermute x50, waiting for transfers between devices, xor_permute(): lax.ppermute(values, axis, [(place, place ^ mask) for place in range(size)])  438 us
    reduce_scatter x4, waiting for transfers between devices, scatter_rows(): lax.psum_scatter(terms.astype(jnp.bfloat16), ('ctx', 'mp'), scatter_dimen...  137 us
    ppermute x50, starting transfers between devices, xor_permute(): lax.ppermute(values, axis, [(place, place ^ mask) for place in range(size)])  72.4 us
    unnamed x224, local copies, waits for them, and re-layouts  54.9 us
    dot_general x9, matrix products, dot_rows(): lax.dot_general(left_mat, right_mat, (((1,), (1,)), ((), ())), preferred_...  45.5 us
    all_gather x1, blocking collectives, per_device_grouped(): segments_all = lax.all_gather(segment_ids, 'ctx', axis=2, tiled=True)  34.3 us
    dot_general x9, matrix products, dot_cols(): lax.dot_general(left_mat, right_mat, (((0,), (0,)), ((), ())), preferred_...  25.6 us
  transfers between devices with their start and end apart: 74, of which 33 were waited for; matrix products, arithmetic and copies ran while one was open for 17% of the time, Pallas kernels for 0%

profile of v1, /device:TPU:0, one launch (start us, length us, event | category | flops | bytes accessed | tf_op | source)
XLA Modules:
  0.0 971.8 jit_solution(17304232157227739559)
XLA Ops:
  38.0 34.3 %all_gather.15 = s32[2,1,1024]{2,1,0:T(1,128)S(1)} all-gather(s32[2,1,256]{2,1,0:T(1,128)S(1)} %copy-done.63), channel_id=1, replica_groups=mesh['dp'=2,'ctx'=4,'mp'=4] {'ctx'}, dimensions={2}, use_global_device_ids=true | all-gather | bytes 10240 | tf_op jit(solution)/shard_map/all_gather | solution.py:452
  111.2 17.4 %collective-permute-done.8 = bf16[256,768]{1,0:T(8,128)(2,1)S(1)} collective-permute-done((bf16[256,768]{1,0:T(8,128)(2,1)S(1)}, bf16[256,768]{1,0:T(8,128)(2,1)S(1)}, u32[]{:S(2)}, u32[]{:S(2)}) %collective-permute-start.8) | collective-permute-done | bytes 393248 | tf_op jit(solution)/shard_map/ppermute | solution.py:341
  150.8 47.9 %reduce-scatter.5.cloned.1.call-done = bf16[128,2048]{1,0:T(8,128)(2,1)} async-done(((bf16[1024,2048]{1,0:T(8,128)(2,1)}), bf16[128,2048]{1,0:T(8,128)(2,1)}) %reduce-scatter.5.cloned.1.call-update) | async-done | bytes 524304 | tf_op jit(solution)/shard_map/reduce_scatter | solution.py:430
  229.9 14.4 %collective-permute-done.18 = bf16[256,1024]{1,0:T(8,128)(2,1)} collective-permute-done((bf16[256,1024]{1,0:T(8,128)(2,1)}, bf16[256,1024]{1,0:T(8,128)(2,1)}, u32[]{:S(2)}, u32[]{:S(2)}) %collective-permute-start.18) | collective-permute-done | bytes 524320 | tf_op jit(solution)/shard_map/ppermute | solution.py:341
  248.5 42.5 %collective-permute-done.19 = bf16[256,1024]{1,0:T(8,128)(2,1)S(1)} collective-permute-done((bf16[256,1024]{1,0:T(8,128)(2,1)}, bf16[256,1024]{1,0:T(8,128)(2,1)S(1)}, u32[]{:S(2)}, u32[]{:S(2)}) %collective-permute-start.19) | collective-permute-done | bytes 524320 | tf_op jit(solution)/shard_map/ppermute | solution.py:341
  297.5 30.8 %collective-permute-done.25 = bf16[256,1024]{1,0:T(8,128)(2,1)S(1)} collective-permute-done((bf16[256,1024]{1,0:T(8,128)(2,1)}, bf16[256,1024]{1,0:T(8,128)(2,1)S(1)}, u32[]{:S(2)}, u32[]{:S(2)}) %collective-permute-start.25) | collective-permute-done | bytes 524320 | tf_op jit(solution)/shard_map/ppermute | solution.py:341
  343.1 21.1 %collective-permute-done.26 = bf16[256,1024]{1,0:T(8,128)(2,1)S(1)} collective-permute-done((bf16[256,1024]{1,0:T(8,128)(2,1)}, bf16[256,1024]{1,0:T(8,128)(2,1)S(1)}, u32[]{:S(2)}, u32[]{:S(2)}) %collective-permute-start.26) | collective-permute-done | bytes 524320 | tf_op jit(solution)/shard_map/ppermute | solution.py:341
  372.3 18.1 %collective-permute-done.36 = bf16[1024,256]{1,0:T(8,128)(2,1)S(1)} collective-permute-done((bf16[1024,256]{1,0:T(8,128)(2,1)}, bf16[1024,256]{1,0:T(8,128)(2,1)S(1)}, u32[]{:S(2)}, u32[]{:S(2)}) %collective-permute-start.36) | collective-permute-done | bytes 524320 | tf_op jit(solution)/shard_map/ppermute | solution.py:341
  391.9 21.0 %collective-permute-done.37 = bf16[1024,256]{1,0:T(8,128)(2,1)S(1)} collective-permute-done((bf16[1024,256]{1,0:T(8,128)(2,1)S(1)}, bf16[1024,256]{1,0:T(8,128)(2,1)S(1)}, u32[]{:S(2)}, u32[]{:S(2)}) %collective-permute-start.37) | collective-permute-done | bytes 524320 | tf_op jit(solution)/shard_map/ppermute | solution.py:341
  415.3 31.3 %collective-permute-done.22 = bf16[256,1024]{1,0:T(8,128)(2,1)S(1)} collective-permute-done((bf16[256,1024]{1,0:T(8,128)(2,1)}, bf16[256,1024]{1,0:T(8,128)(2,1)S(1)}, u32[]{:S(2)}, u32[]{:S(2)}) %collective-permute-start.22) | collective-permute-done | bytes 524320 | tf_op jit(solution)/shard_map/ppermute | solution.py:341
  448.1 9.7 %collective-permute-done.23 = bf16[256,1024]{1,0:T(8,128)(2,1)S(1)} collective-permute-done((bf16[256,1024]{1,0:T(8,128)(2,1)S(1)}, bf16[256,1024]{1,0:T(8,128)(2,1)S(1)}, u32[]{:S(2)}, u32[]{:S(2)}) %collective-permute-start.23) | collective-permute-done | bytes 524320 | tf_op jit(solution)/shard_map/ppermute | solution.py:341
  476.4 10.1 %fusion.70 = f32[1024,1024]{1,0:T(8,128)} fusion(bf16[1024,2048]{1,0:T(8,128)(2,1)} %all-gather.7.cloned.1.call-done, bf16[2048,1024]{1,0:T(8,128)(2,1)} %bitcast_dynamic-update-slice_fusion.16), kind=kOutput, calls=%fused_computation.328 | convolution fusion | flops 4294967296 | bytes 12582912 | tf_op jit(solution)/shard_map/dot_general | solution.py:509
  492.9 14.0 %multiply_convert_fusion.2 = (bf16[1024,1024]{1,0:T(8,128)(2,1)}, bf16[1024,1024]{1,0:T(8,128)(2,1)S(1)}, bf16[1024,1024]{1,0:T(8,128)(2,1)}) fusion(f32[1024,1024]{1,0:T(8,128)} %fusion.69, f32[1024,1024]{1,0:T(8,128)} %fusion.70, bf16[1024,2048]{1,0:T(8,128)(2,1)} %all-gather.9.cloned.1.call-done, bf16[1024,2048]{1,0:T(8,128)(2,1)} %copy-done.54), kind=kOutput, calls=%fused_computation.13 | convolution fusion | flops 4311744512 | bytes 23068672 | tf_op jit(solution)/shard_map/dot_general | solution.py:52
  511.6 9.6 add_convert_fusion
  521.2 9.3 convolution_convert_fusion.2
  530.6 39.0 %reduce-scatter.9.cloned.1.call-done = bf16[128,2048]{1,0:T(8,128)(2,1)} async-done(((bf16[1024,2048]{1,0:T(8,128)(2,1)}), bf16[128,2048]{1,0:T(8,128)(2,1)}) %reduce-scatter.9.cloned.1.call-update) | async-done | bytes 524304 | tf_op jit(solution)/shard_map/reduce_scatter | solution.py:430
  571.1 50.0 %reduce-scatter.7.cloned.1.call-done = bf16[128,2048]{1,0:T(8,128)(2,1)} async-done(((bf16[1024,2048]{1,0:T(8,128)(2,1)}), bf16[128,2048]{1,0:T(8,128)(2,1)}) %reduce-scatter.7.cloned.1.call-update) | async-done | bytes 524304 | tf_op jit(solution)/shard_map/reduce_scatter | solution.py:430
  652.9 26.1 %collective-permute-done.63 = bf16[1024,1024]{1,0:T(8,128)(2,1)S(1)} collective-permute-done((bf16[1024,1024]{1,0:T(8,128)(2,1)S(1)}, bf16[1024,1024]{1,0:T(8,128)(2,1)S(1)}, u32[]{:S(2)}, u32[]{:S(2)}) %collective-permute-start.63) | collective-permute-done | bytes 2097184 | tf_op jit(solution)/shard_map/ppermute | solution.py:341
  709.8 14.3 %collective-permute-done.60 = bf16[1024,1024]{0,1:T(8,128)(2,1)} collective-permute-done((bf16[1024,1024]{0,1:T(8,128)(2,1)}, bf16[1024,1024]{0,1:T(8,128)(2,1)}, u32[]{:S(2)}, u32[]{:S(2)}) %collective-permute-start.60) | collective-permute-done | bytes 2097184 | tf_op jit(solution)/shard_map/ppermute | solution.py:341
  731.3 37.8 %collective-permute-done.57 = bf16[1024,1024]{0,1:T(8,128)(2,1)} collective-permute-done((bf16[1024,1024]{0,1:T(8,128)(2,1)S(1)}, bf16[1024,1024]{0,1:T(8,128)(2,1)}, u32[]{:S(2)}, u32[]{:S(2)}) %collective-permute-start.57) | collective-permute-done | bytes 2097184 | tf_op jit(solution)/shard_map/ppermute | solution.py:341
  783.4 40.4 %collective-permute-done.58 = bf16[512,1024]{0,1:T(8,128)(2,1)S(1)} collective-permute-done((bf16[512,1024]{0,1:T(8,128)(2,1)S(1)}, bf16[512,1024]{0,1:T(8,128)(2,1)S(1)}, u32[]{:S(2)}, u32[]{:S(2)}) %collective-permute-start.58) | collective-permute-done | bytes 1048608 | tf_op jit(solution)/shard_map/ppermute | solution.py:341
  847.2 33.6 %collective-permute-done.54 = bf16[256,1024]{0,1:T(8,128)(2,1)} collective-permute-done((bf16[256,1024]{0,1:T(8,128)(2,1)}, bf16[256,1024]{0,1:T(8,128)(2,1)}, u32[]{:S(2)}, u32[]{:S(2)}) %collective-permute-start.54) | collective-permute-done | bytes 524320 | tf_op jit(solution)/shard_map/ppermute | solution.py:341
  901.1 17.0 %collective-permute-done.55 = bf16[256,512]{0,1:T(8,128)(2,1)} collective-permute-done((bf16[256,512]{0,1:T(8,128)(2,1)}, bf16[256,512]{0,1:T(8,128)(2,1)}, u32[]{:S(2)}, u32[]{:S(2)}) %collective-permute-start.55) | collective-permute-done | bytes 262176 | tf_op jit(solution)/shard_map/ppermute | solution.py:341
  919.2 14.6 %collective-permute-done.52 = bf16[512,768]{0,1:T(8,128)(2,1)} collective-permute-done((bf16[512,768]{0,1:T(8,128)(2,1)S(1)}, bf16[512,768]{0,1:T(8,128)(2,1)}, u32[]{:S(2)}, u32[]{:S(2)}) %collective-permute-start.52) | collective-permute-done | bytes 786464 | tf_op jit(solution)/shard_map/ppermute | solution.py:341
  (502 shorter events, 351.2 us)
Async XLA Ops:
  7.2 127.7 %all-gather.5.cloned.1.call-start = ((), (), s32[]{:S(2)}) async-start(), calls=%async_computation.4 | async-start | bytes 4718592 | tf_op jit(solution)/shard_map/all_gather | solution.py:426
  23.7 175.0 %reduce-scatter.5.cloned.1.call-start = ((), (), s32[]{:S(2)}) async-start(), calls=%async_computation.5 | async-start | bytes 4718592 | tf_op jit(solution)/shard_map/reduce_scatter | solution.py:430
  23.8 58.7 %collective-permute-start.13 = (bf16[256,256]{1,0:T(8,128)(2,1)S(1)}, bf16[256,256]{1,0:T(8,128)(2,1)S(1)}, u32[]{:S(2)}, u32[]{:S(2)}) collective-permute-start(bf16[256,256]{1,0:T(8,128)(2,1)S(1)} %constant_dynamic-slice_fusion.16), channel_id=1, source_target_pairs={{0,12},{4,8},{8,4},{12,0},{1,13},{5,9},{9,5},{13,1},{2,14},{6,10},... | collective-permute-start | bytes 393224 | tf_op jit(solution)/shard_map/ppermute | solution.py:341
  32.8 72.6 %collective-permute-start.5 = (bf16[256,768]{1,0:T(8,128)(2,1)}, bf16[256,768]{1,0:T(8,128)(2,1)S(1)}, u32[]{:S(2)}, u32[]{:S(2)}) collective-permute-start(bf16[256,768]{1,0:T(8,128)(2,1)} %pad_maximum_fusion.23), channel_id=1, source_target_pairs={{0,8},{4,12},{8,0},{12,4},{1,9},{5,13},{9,1},{13,5},{2,10},{6,14},... | collective-permute-start | bytes 1179656 | tf_op jit(solution)/shard_map/ppermute | solution.py:341
  34.2 75.9 %collective-permute-start.7 = (bf16[256,768]{1,0:T(8,128)(2,1)}, bf16[256,768]{1,0:T(8,128)(2,1)}, u32[]{:S(2)}, u32[]{:S(2)}) collective-permute-start(bf16[256,768]{1,0:T(8,128)(2,1)} %pad_maximum_fusion.23), channel_id=1, source_target_pairs={{0,16},{16,0},{1,17},{17,1},{2,18},{18,2},{3,19},{19,3},{4,20},{20... | collective-permute-start | bytes 1179656 | tf_op jit(solution)/shard_map/ppermute | solution.py:341
  36.5 70.5 %collective-permute-start.6 = (bf16[256,768]{1,0:T(8,128)(2,1)}, bf16[256,768]{1,0:T(8,128)(2,1)}, u32[]{:S(2)}, u32[]{:S(2)}) collective-permute-start(bf16[256,768]{1,0:T(8,128)(2,1)} %pad_maximum_fusion.24), channel_id=1, source_target_pairs={{0,12},{4,8},{8,4},{12,0},{1,13},{5,9},{9,5},{13,1},{2,14},{6,10},... | collective-permute-start | bytes 1179656 | tf_op jit(solution)/shard_map/ppermute | solution.py:341
  150.8 325.6 %all-gather.7.cloned.1.call-start = ((), (), s32[]{:S(2)}) async-start(), calls=%async_computation.6 | async-start | bytes 4718592 | tf_op jit(solution)/shard_map/all_gather | solution.py:426
  203.4 289.5 %all-gather.9.cloned.1.call-start = ((), (), s32[]{:S(2)}) async-start(), calls=%async_computation.8 | async-start | bytes 4718592 | tf_op jit(solution)/shard_map/all_gather | solution.py:426
  220.7 120.7 %collective-permute-start.34 = (bf16[1024,256]{1,0:T(8,128)(2,1)}, bf16[1024,256]{1,0:T(8,128)(2,1)}, u32[]{:S(2)}, u32[]{:S(2)}) collective-permute-start(bf16[1024,256]{1,0:T(8,128)(2,1)} %constant_dynamic-slice_fusion.10), channel_id=1, source_target_pairs={{0,12},{4,8},{8,4},{12,0},{1,13},{5,9},{9,5},{13,1},{2,14},{6,10},... | collective-permute-start | bytes 1572872 | tf_op jit(solution)/shard_map/ppermute | solution.py:341
  223.1 107.5 %collective-permute-start.32 = (bf16[1024,256]{1,0:T(8,128)(2,1)}, bf16[1024,256]{1,0:T(8,128)(2,1)}, u32[]{:S(2)}, u32[]{:S(2)}) collective-permute-start(bf16[1024,256]{1,0:T(8,128)(2,1)} %constant_dynamic-slice_fusion.10), channel_id=1, source_target_pairs={{0,4},{4,0},{8,12},{12,8},{1,5},{5,1},{9,13},{13,9},{2,6},{6,2},{1... | collective-permute-start | bytes 1572872 | tf_op jit(solution)/shard_map/ppermute | solution.py:341
  223.8 70.5 %collective-permute-start.20 = (bf16[256,1024]{1,0:T(8,128)(2,1)}, bf16[256,1024]{1,0:T(8,128)(2,1)S(1)}, u32[]{:S(2)}, u32[]{:S(2)}) collective-permute-start(bf16[256,1024]{1,0:T(8,128)(2,1)} %constant_dynamic-slice_fusion.14), channel_id=1, source_target_pairs={{0,12},{4,8},{8,4},{12,0},{1,13},{5,9},{9,5},{13,1},{2,14},{6,10},... | collective-permute-start | bytes 1572872 | tf_op jit(solution)/shard_map/ppermute | solution.py:341
  224.8 66.3 %collective-permute-start.19 = (bf16[256,1024]{1,0:T(8,128)(2,1)}, bf16[256,1024]{1,0:T(8,128)(2,1)S(1)}, u32[]{:S(2)}, u32[]{:S(2)}) collective-permute-start(bf16[256,1024]{1,0:T(8,128)(2,1)} %get-tuple-element.36), channel_id=1, source_target_pairs={{0,8},{4,12},{8,0},{12,4},{1,9},{5,13},{9,1},{13,5},{2,10},{6,14},... | collective-permute-start | bytes 1572872 | tf_op jit(solution)/shard_map/ppermute | solution.py:341
  229.8 339.7 %reduce-scatter.9.cloned.1.call-start = ((), (), s32[]{:S(2)}) async-start(), calls=%async_computation.9 | async-start | bytes 4718592 | tf_op jit(solution)/shard_map/reduce_scatter | solution.py:430
  244.3 84.0 %collective-permute-start.25 = (bf16[256,1024]{1,0:T(8,128)(2,1)}, bf16[256,1024]{1,0:T(8,128)(2,1)S(1)}, u32[]{:S(2)}, u32[]{:S(2)}) collective-permute-start(bf16[256,1024]{1,0:T(8,128)(2,1)} %constant_dynamic-slice_fusion.12), channel_id=1, source_target_pairs={{0,4},{4,0},{8,12},{12,8},{1,5},{5,1},{9,13},{13,9},{2,6},{6,2},{1... | collective-permute-start | bytes 1572872 | tf_op jit(solution)/shard_map/ppermute | solution.py:341
  291.1 75.4 %collective-permute-start.27 = (bf16[256,1024]{1,0:T(8,128)(2,1)}, bf16[256,1024]{1,0:T(8,128)(2,1)S(1)}, u32[]{:S(2)}, u32[]{:S(2)}) collective-permute-start(bf16[256,1024]{1,0:T(8,128)(2,1)} %constant_dynamic-slice_fusion.12), channel_id=1, source_target_pairs={{0,12},{4,8},{8,4},{12,0},{1,13},{5,9},{9,5},{13,1},{2,14},{6,10},... | collective-permute-start | bytes 1572872 | tf_op jit(solution)/shard_map/ppermute | solution.py:341
  367.8 99.5 %collective-permute-start.31 = (bf16[256,1024]{1,0:T(8,128)(2,1)S(1)}, bf16[256,1024]{1,0:T(8,128)(2,1)S(1)}, u32[]{:S(2)}, u32[]{:S(2)}) collective-permute-start(bf16[256,1024]{1,0:T(8,128)(2,1)S(1)} %collective-permute-done.27), channel_id=1, source_target_pairs={{0,16},{16,0},{1,17},{17,1},{2,18},{18,2},{3,19},{19,3},{4,20},{20... | collective-permute-start | bytes 1572872 | tf_op jit(solution)/shard_map/ppermute | solution.py:341
  370.8 87.5 %collective-permute-start.29 = (bf16[256,1024]{1,0:T(8,128)(2,1)S(1)}, bf16[256,1024]{1,0:T(8,128)(2,1)S(1)}, u32[]{:S(2)}, u32[]{:S(2)}) collective-permute-start(bf16[256,1024]{1,0:T(8,128)(2,1)S(1)} %collective-permute-done.25), channel_id=1, source_target_pairs={{0,16},{16,0},{1,17},{17,1},{2,18},{18,2},{3,19},{19,3},{4,20},{20... | collective-permute-start | bytes 1572872 | tf_op jit(solution)/shard_map/ppermute | solution.py:341
  390.4 67.5 %collective-permute-start.24 = (bf16[256,1024]{1,0:T(8,128)(2,1)S(1)}, bf16[256,1024]{1,0:T(8,128)(2,1)S(1)}, u32[]{:S(2)}, u32[]{:S(2)}) collective-permute-start(bf16[256,1024]{1,0:T(8,128)(2,1)S(1)} %collective-permute-done.20), channel_id=1, source_target_pairs={{0,16},{16,0},{1,17},{17,1},{2,18},{18,2},{3,19},{19,3},{4,20},{20... | collective-permute-start | bytes 1572872 | tf_op jit(solution)/shard_map/ppermute | solution.py:341
  521.2 99.9 %reduce-scatter.7.cloned.1.call-start = ((), (), s32[]{:S(2)}) async-start(), calls=%async_computation.7 | async-start | bytes 4718592 | tf_op jit(solution)/shard_map/reduce_scatter | solution.py:430
  530.5 154.7 %all-gather.11.cloned.1.call-start = ((), (), s32[]{:S(2)}) async-start(), calls=%async_computation.10 | async-start | bytes 4718592 | tf_op jit(solution)/shard_map/all_gather | solution.py:426
  624.3 323.1 %reduce-scatter.11.cloned.1.call-start = ((), (), s32[]{:S(2)}) async-start(), calls=%async_computation.11 | async-start | bytes 4718592 | tf_op jit(solution)/shard_map/reduce_scatter | solution.py:430
  643.3 80.8 %collective-permute-start.60 = (bf16[1024,1024]{0,1:T(8,128)(2,1)}, bf16[1024,1024]{0,1:T(8,128)(2,1)}, u32[]{:S(2)}, u32[]{:S(2)}) collective-permute-start(bf16[1024,1024]{0,1:T(8,128)(2,1)} %dynamic-slice_convert_fusion.1), channel_id=1, source_target_pairs={{0,16},{16,0},{1,17},{17,1},{2,18},{18,2},{3,19},{19,3},{4,20},{20... | collective-permute-start | bytes 6291464 | tf_op jit(solution)/shard_map/ppermute | solution.py:341
  649.9 119.1 %collective-permute-start.57 = (bf16[1024,1024]{0,1:T(8,128)(2,1)S(1)}, bf16[1024,1024]{0,1:T(8,128)(2,1)}, u32[]{:S(2)}, u32[]{:S(2)}) collective-permute-start(bf16[1024,1024]{0,1:T(8,128)(2,1)S(1)} %dynamic-slice_convert_fusion.2), channel_id=1, source_target_pairs={{0,16},{16,0},{1,17},{17,1},{2,18},{18,2},{3,19},{19,3},{4,20},{20... | collective-permute-start | bytes 6291464 | tf_op jit(solution)/shard_map/ppermute | solution.py:341
  682.8 94.2 %collective-permute-start.64 = (bf16[1024,512]{1,0:T(8,128)(2,1)}, bf16[1024,512]{1,0:T(8,128)(2,1)}, u32[]{:S(2)}, u32[]{:S(2)}) collective-permute-start(bf16[1024,512]{1,0:T(8,128)(2,1)} %dynamic-slice_convert_fusion.4), channel_id=1, source_target_pairs={{0,8},{4,12},{8,0},{12,4},{1,9},{5,13},{9,1},{13,5},{2,10},{6,14},... | collective-permute-start | bytes 3145736 | tf_op jit(solution)/shard_map/ppermute | solution.py:341
  (121 other events, 2477.9 us)
Sparse Core Ops, SparseCore 0:
  23.8 50.1 all-gather.4
  150.9 47.7 reduce-scatter.4
  203.6 81.5 all-gather.6
  287.2 59.5 all-gather.8
  521.3 48.2 reduce-scatter.8
  571.7 49.3 reduce-scatter.6
  624.5 31.1 all-gather.10
  709.9 75.8 reduce-scatter.10

commit v2 on v1

--- a/solution.py
+++ b/solution.py
@@ -3,6 +3,8 @@
 import jax
 import jax.numpy as jnp
 from jax import lax
+from jax.experimental import pallas as pl
+from jax.experimental.pallas import tpu as pltpu
 from jax.sharding import PartitionSpec as P
 
 HD = 128
@@ -337,6 +339,530 @@
     )
 
 
+MESH = pl.DeviceIdType.MESH
+HBM = pl.BlockSpec(memory_space=pl.ANY)
+LOW = jnp.bfloat16
+FULL = jnp.float32
+TILE = 256
+
+
+def contract(left, right, left_dim, right_dim):
+    return lax.dot_general(
+        left, right, (((left_dim,), (right_dim,)), ((), ())), preferred_element_type=FULL
+    )
+
+
+def aligned(start, size, unit=None):
+    return pl.ds(pl.multiple_of(start, size if unit is None else unit), size)
+
+
+class Place:
+    def __init__(self):
+        self.dp = lax.axis_index("dp")
+        self.ctx = lax.axis_index("ctx")
+        self.mp = lax.axis_index("mp")
+        self.high = self.ctx // 2
+        self.low = self.ctx % 2
+        self.chip = self.mp // 2
+        self.core = self.mp % 2
+        self.home = self.dp * 4 + self.ctx
+
+    def along(self, mask):
+        other = self.ctx + mask - 2 * (self.ctx & mask)
+        return (self.dp, other, self.mp)
+
+    def across(self):
+        return (1 - self.dp, self.ctx, self.mp)
+
+    def beside_chip(self):
+        return (self.dp, self.ctx, (1 - self.chip) * 2 + self.core)
+
+    def beside_core(self):
+        return (self.dp, self.ctx, self.chip * 2 + 1 - self.core)
+
+    def shard_rows(self, low, chip, core, size=128):
+        return aligned((core * 4 + chip * 2 + low) * 128, size, 128)
+
+
+class Mover:
+    def __init__(self, send, receive, local):
+        self.send, self.receive, self.local = send, receive, local
+        self.remote_count = 0
+        self.local_count = 0
+
+    def to(self, source, target, device):
+        slot = self.remote_count
+        self.remote_count += 1
+        copy = pltpu.make_async_remote_copy(
+            src_ref=source,
+            dst_ref=target,
+            send_sem=self.send.at[slot],
+            recv_sem=self.receive.at[slot],
+            device_id=device,
+            device_id_type=MESH,
+        )
+        copy.start()
+        return copy
+
+    def here(self, source, target):
+        slot = self.local_count
+        self.local_count += 1
+        copy = pltpu.make_async_copy(source, target, self.local.at[slot])
+        copy.start()
+        return copy
+
+
+def greet(partners):
+    barrier = pltpu.get_barrier_semaphore()
+    for partner in partners:
+        pl.semaphore_signal(barrier, inc=1, device_id=partner, device_id_type=MESH)
+    pl.semaphore_wait(barrier, len(partners))
+
+
+class GroupGather:
+    def __init__(self, place, mover, view, own):
+        self.place, self.mover, self.view = place, mover, view
+        p = place
+        landing = view(p.low, p.chip, p.core)
+        self.along = mover.to(own, landing, p.along(1))
+        self.chip = mover.to(own, landing, p.beside_chip())
+        self.core = mover.to(own, landing, p.beside_core())
+        self.sent = [self.along, self.chip, self.core]
+
+    def relay_along(self):
+        p = self.place
+        self.along.wait_recv()
+        piece = self.view(1 - p.low, p.chip, p.core)
+        self.corner = self.mover.to(piece, piece, p.beside_chip())
+        self.along_core = self.mover.to(piece, piece, p.beside_core())
+        self.sent += [self.corner, self.along_core]
+
+    def relay_chip(self):
+        p = self.place
+        self.chip.wait_recv()
+        piece = self.view(p.low, 1 - p.chip, p.core)
+        self.chip_core = self.mover.to(piece, piece, p.beside_core())
+        self.sent.append(self.chip_core)
+
+    def relay_corner(self):
+        p = self.place
+        self.corner.wait_recv()
+        piece = self.view(1 - p.low, 1 - p.chip, p.core)
+        self.corner_core = self.mover.to(piece, piece, p.beside_core())
+        self.sent.append(self.corner_core)
+
+    def finish(self):
+        for copy in (self.core, self.along_core, self.chip_core, self.corner_core):
+            copy.wait_recv()
+        for copy in self.sent:
+            copy.wait_send()
+
+
+class GroupScatter:
+    def __init__(self, place, mover, buffers, terms):
+        self.place, self.mover, self.buffers, self.terms = place, mover, buffers, terms
+        self.sent = []
+
+    def half(self, part):
+        return pl.ds(part * TILE, TILE)
+
+    def rows(self, chip, core):
+        return self.place.shard_rows(0, chip, core, TILE)
+
+    def start_core(self, part):
+        p = self.place
+        core_send, core_recv = self.buffers[:2]
+        chip = 1 - p.chip if part == 0 else p.chip
+        core_send[self.half(part), :] = self.terms(self.rows(chip, 1 - p.core)).astype(LOW)
+        copy = self.mover.to(
+            core_send.at[self.half(part)], core_recv.at[self.half(part)], p.beside_core()
+        )
+        self.sent.append(copy)
+        if part == 0:
+            self.core_first = copy
+        else:
+            self.core_second = copy
+
+    def start_chip(self):
+        p = self.place
+        core_recv, chip_send, chip_recv = self.buffers[1:4]
+        total = self.terms(self.rows(1 - p.chip, p.core))
+        self.core_first.wait_recv()
+        chip_send[...] = (total + core_recv[self.half(0), :].astype(FULL)).astype(LOW)
+        self.chip_copies = []
+        for which in (1 - p.low, p.low):
+            rows = aligned(which * 128, 128)
+            self.chip_copies.append(
+                self.mover.to(chip_send.at[rows], chip_recv.at[rows], p.beside_chip())
+            )
+        self.sent += self.chip_copies
+
+    def start_along(self):
+        p = self.place
+        core_recv, _, chip_recv, along_send, along_recv, total_ref = self.buffers[1:]
+        total = self.terms(self.rows(p.chip, p.core))
+        self.core_second.wait_recv()
+        total_ref[...] = total + core_recv[self.half(1), :].astype(FULL)
+        self.chip_copies[0].wait_recv()
+        rows = aligned((1 - p.low) * 128, 128)
+        along_send[...] = (total_ref[rows, :] + chip_recv[rows, :].astype(FULL)).astype(LOW)
+        self.along = self.mover.to(along_send, along_recv, p.along(1))
+        self.sent.append(self.along)
+
+    def result(self):
+        p = self.place
+        chip_recv, _, along_recv, total_ref = self.buffers[3:]
+        self.chip_copies[1].wait_recv()
+        rows = aligned(p.low * 128, 128)
+        total = total_ref[rows, :] + chip_recv[rows, :].astype(FULL)
+        self.along.wait_recv()
+        total = total + along_recv[...].astype(FULL)
+        for copy in self.sent:
+            copy.wait_send()
+        return total
+
+
+def scatter_buffers(width):
+    return [
+        pltpu.VMEM((2 * TILE, width), LOW),
+        pltpu.VMEM((2 * TILE, width), LOW),
+        pltpu.VMEM((TILE, width), LOW),
+        pltpu.VMEM((TILE, width), LOW),
+        pltpu.VMEM((TILE // 2, width), LOW),
+        pltpu.VMEM((TILE // 2, width), LOW),
+        pltpu.VMEM((TILE, width), FULL),
+    ]
+
+
+class WeightFetch:
+    def __init__(self, place, mover, shard, whole, axis, start, size, landing):
+        self.place, self.mover = place, mover
+        half = shard.shape[axis] // 2
+        block = shard.shape[1 - axis]
+
+        def source(which):
+            part = aligned(which * half + start, size, 128)
+            return shard.at[:, part] if axis == 1 else shard.at[part, :]
+
+        def target(ctx):
+            span = aligned((place.dp * 4 + ctx) * block, block, 128)
+            part = pl.ds(landing, size)
+            return whole.at[span, part] if axis == 1 else whole.at[part, span]
+
+        self.source, self.target = source, target
+
+    def start(self):
+        p = self.place
+        mine = self.source(p.low)
+        other = self.source(1 - p.low)
+        spot = self.target(p.ctx)
+        self.near = [
+            self.mover.to(mine, spot, p.along(2)),
+            self.mover.to(other, spot, p.along(3)),
+            self.mover.to(other, spot, p.along(1)),
+        ]
+        self.local = self.mover.here(mine, spot)
+
+    def cross(self):
+        p = self.place
+        self.far = [self.mover.to(self.source(p.low), self.target(p.ctx), p.across())]
+        for copy, mask in ((self.near[2], 1), (self.near[0], 2), (self.near[1], 3)):
+            copy.wait_recv()
+            block = self.target(p.along(mask)[1])
+            self.far.append(self.mover.to(block, block, p.across()))
+
+    def finish(self):
+        self.local.wait()
+        for copy in self.far:
+            copy.wait_recv()
+
+    def drain(self):
+        for copy in self.near + self.far:
+            copy.wait_send()
+
+
+def normalise(values):
+    centred = values - jnp.mean(values, axis=-1, keepdims=True)
+    inverse = lax.rsqrt(jnp.mean(centred * centred, axis=-1, keepdims=True) + EPSILON)
+    return centred * inverse, inverse
+
+
+def allowed_mask(seg_col, seg_row, start, keys):
+    rows = seg_col[pl.ds(start, TILE), :][:, :1]
+    cols = seg_row[0:1, pl.ds(0, keys)]
+    row_place = start + lax.broadcasted_iota(jnp.int32, (TILE, keys), 0)
+    col_place = lax.broadcasted_iota(jnp.int32, (TILE, keys), 1)
+    return (rows == cols) & (col_place <= row_place)
+
+
+def turn(values, cosine, sine_part):
+    parts = []
+    for start in range(0, values.shape[1], HD):
+        head = values[:, start : start + HD]
+        parts.append(head * cosine + pltpu.roll(head, HD // 2, 1) * sine_part)
+    return jnp.concatenate(parts, axis=1)
+
+
+def attention_kernel(
+    tokens_in, out_grad, seg_col_in, seg_row_in, freqs, w_query, w_key, w_value, w_out, w_gate, w_up, w_down,
+    qkv_all, out_all, gate_all, up_all, down_all, grads_all, second_all, normed_out,
+    query, key, value, mixed, log_total, cosine, sine_part, seg_col, seg_row, residual, inverse_two, kept,
+    tokens, qkv_here, out_here, second_rows, core_send, core_recv, chip_send, chip_recv, along_send, along_recv,
+    total_ref, send, receive, local,
+):
+    p = Place()
+    mover = Mover(send, receive, local)
+    greet([p.along(1), p.along(2), p.along(3), p.across(), p.beside_chip(), p.beside_core()])
+    length, width = tokens.shape
+    span, feats = tokens_in.shape[2:]
+    cols = w_query.shape[1] // 2
+    score_scale = 1.0 / math.sqrt(HD)
+
+    def fetch(shard, whole, axis, landing=0, pieces=1):
+        size = shard.shape[axis] // 2 // pieces
+        return [
+            WeightFetch(p, mover, shard, whole, axis, piece * size, size, landing + piece * size)
+            for piece in range(pieces)
+        ]
+
+    fetch_query = fetch(w_query, qkv_all, 1, 0)
+    fetch_key = fetch(w_key, qkv_all, 1, cols)
+    fetch_value = fetch(w_value, qkv_all, 1, 2 * cols)
+    fetch_out = fetch(w_out, out_all, 0)
+    fetch_gate = fetch(w_gate, gate_all, 1, 0, 2)
+    fetch_up = fetch(w_up, up_all, 1, 0, 2)
+    fetch_down = fetch(w_down, down_all, 0, 0, 2)
+
+    def block_of(whole, ctx, model):
+        return whole.at[aligned(ctx * span, span), aligned(model * feats, feats)]
+
+    def own_view(whole):
+        return lambda low, chip, core: block_of(whole, p.high * 2 + low, chip * 2 + core)
+
+    def other_view(whole):
+        return lambda low, chip, core: block_of(whole, (1 - p.high) * 2 + low, chip * 2 + core)
+
+    seg_copies = []
+    for mask in (1, 2, 3):
+        goal = p.high if mask == 1 else 1 - p.high
+        spot = aligned(p.ctx * span, span)
+        seg_copies.append(mover.to(seg_col_in.at[goal], seg_col.at[spot], p.along(mask)))
+        seg_copies.append(mover.to(seg_row_in.at[goal], seg_row.at[:, spot], p.along(mask)))
+    seg_local = [
+        mover.here(seg_col_in.at[p.high], seg_col.at[aligned(p.ctx * span, span)]),
+        mover.here(seg_row_in.at[p.high], seg_row.at[:, aligned(p.ctx * span, span)]),
+    ]
+    here = block_of(tokens, p.ctx, p.mp)
+    swap = mover.to(tokens_in.at[1 - p.high, 0], here, p.along(2))
+    own_tokens = tokens_in.at[p.high, 0]
+    tokens_local = mover.here(own_tokens, here)
+    gather_own = GroupGather(p, mover, own_view(tokens), own_tokens)
+    for chunk in fetch_query + fetch_key:
+        chunk.start()
+    for copy in seg_copies:
+        copy.wait()
+    for copy in seg_local:
+        copy.wait()
+    for start in range(0, length, TILE):
+        rows = pl.ds(start, TILE)
+        keys = start + TILE
+        allowed = allowed_mask(seg_col, seg_row, start, keys)
+        position = jnp.sum(jnp.where(allowed, 1.0, 0.0), axis=1, keepdims=True) - 1.0
+        angle = position * freqs[0:1, :]
+        cosine[rows, :] = jnp.cos(angle)
+        lane = lax.broadcasted_iota(jnp.int32, (TILE, HD), 1)
+        sine = jnp.sin(angle)
+        sine_part[rows, :] = jnp.where(lane < HD // 2, -sine, sine)
+    swap.wait_recv()
+    gather_other = GroupGather(
+        p, mover, other_view(tokens), block_of(tokens, p.along(2)[1], p.mp)
+    )
+    fetch_value[0].start()
+    gather_own.relay_along()
+    gather_own.relay_chip()
+    gather_own.relay_corner()
+    fetch_query[0].cross()
+    gather_other.relay_along()
+    gather_other.relay_chip()
+    gather_other.relay_corner()
+    fetch_out[0].start()
+    fetch_key[0].cross()
+    tokens_local.wait()
+    swap.wait_send()
+    gather_own.finish()
+    gather_other.finish()
+    my_rows = p.shard_rows(p.low, p.chip, p.core)
+    kept[...] = tokens[my_rows, :]
+    residual[...] = kept[...].astype(FULL)
+    for start in range(0, length, 128):
+        rows = pl.ds(start, 128)
+        tokens[rows, :] = normalise(tokens[rows, :].astype(FULL))[0].astype(LOW)
+    normed_copy = mover.here(tokens, normed_out)
+    fetch_value[0].cross()
+    fetch_gate[0].start()
+    for chunk in fetch_query + fetch_key + fetch_value:
+        chunk.finish()
+    qkv_copy = mover.here(qkv_all, qkv_here)
+    qkv_copy.wait()
+    for start in range(0, length, TILE):
+        rows = pl.ds(start, TILE)
+        three = contract(tokens[rows, :], qkv_here[...], 1, 0)
+        query[rows, :] = turn(three[:, :cols], cosine[rows, :], sine_part[rows, :]).astype(LOW)
+        key[rows, :] = turn(three[:, cols : 2 * cols], cosine[rows, :], sine_part[rows, :]).astype(
+            LOW
+        )
+        value[rows, :] = three[:, 2 * cols :].astype(LOW)
+
+    grads = {}
+
+    def grad_start():
+        spot = block_of(grads_all, p.ctx, p.mp)
+        own = out_grad.at[p.high, 0]
+        grads["swap"] = mover.to(out_grad.at[1 - p.high, 0], spot, p.along(2))
+        grads["local"] = mover.here(own, spot)
+        grads["own"] = GroupGather(p, mover, own_view(grads_all), own)
+
+    def grad_second():
+        grads["swap"].wait_recv()
+        grads["other"] = GroupGather(
+            p, mover, other_view(grads_all), block_of(grads_all, p.along(2)[1], p.mp)
+        )
+
+    pending = [
+        fetch_out[0].cross,
+        grad_start,
+        fetch_gate[1].start,
+        grad_second,
+        fetch_gate[0].cross,
+        lambda: (grads["own"].relay_along(), grads["own"].relay_chip()),
+        fetch_up[0].start,
+        lambda: (grads["own"].relay_corner(), grads["other"].relay_along()),
+        lambda: (grads["other"].relay_chip(), grads["other"].relay_corner()),
+        fetch_gate[1].cross,
+        fetch_up[1].start,
+        fetch_up[0].cross,
+        fetch_down[0].start,
+        fetch_up[1].cross,
+        fetch_down[1].start,
+        fetch_down[0].cross,
+        fetch_down[1].cross,
+    ]
+
+    def pump(count=1):
+        for _ in range(min(count, len(pending))):
+            pending.pop(0)()
+
+    head_count = cols // HD
+    for start in range(0, length, TILE):
+        rows = pl.ds(start, TILE)
+        keys = start + TILE
+        allowed = allowed_mask(seg_col, seg_row, start, keys)
+        for head in range(head_count):
+            head_cols = pl.ds(head * HD, HD)
+            scores = contract(query[rows, head_cols], key[pl.ds(0, keys), head_cols], 1, 1)
+            scores = jnp.where(allowed, scores * score_scale, NEG_FILL)
+            highest = jnp.max(scores, axis=-1, keepdims=True)
+            exp_terms = jnp.exp(scores - highest)
+            total_exp = jnp.sum(exp_terms, axis=-1, keepdims=True)
+            probs_low = (exp_terms * (1.0 / total_exp)).astype(LOW)
+            mixed[rows, head_cols] = contract(
+                probs_low, value[pl.ds(0, keys), head_cols], 1, 0
+            ).astype(LOW)
+            log_total[rows, head_cols] = jnp.broadcast_to(
+                highest + jnp.log(total_exp), (TILE, HD)
+            )
+        pump()
+    fetch_out[0].finish()
+    out_copy = mover.here(out_all, out_here)
+    out_copy.wait()
+    scatter = GroupScatter(
+        p,
+        mover,
+        (core_send, core_recv, chip_send, chip_recv, along_send, along_recv, total_ref),
+        lambda rows: contract(mixed[rows, :], out_here[...], 1, 0),
+    )
+    scatter.start_core(0)
+    scatter.start_core(1)
+    scatter.start_chip()
+    pump()
+    scatter.start_along()
+    pump()
+    branch = scatter.result()
+    hidden = residual[...] + branch
+    residual[...] = hidden
+    normed_two, inverse = normalise(hidden)
+    inverse_two[...] = jnp.broadcast_to(inverse, inverse_two.shape)
+    second_rows[...] = normed_two.astype(LOW)
+
+    def row_view(low, chip, core):
+        return second_all.at[p.shard_rows(low, chip, core)]
+
+    second_local = mover.here(second_rows, row_view(p.low, p.chip, p.core))
+    gather = GroupGather(p, mover, row_view, second_rows)
+    pump(2)
+    gather.relay_along()
+    gather.relay_chip()
+    pump(2)
+    gather.relay_corner()
+    pump(len(pending))
+    for piece in (gather, grads["own"], grads["other"]):
+        piece.finish()
+    second_local.wait()
+    grads["swap"].wait_send()
+    grads["local"].wait()
+    normed_copy.wait()
+    for chunk in fetch_gate + fetch_up + fetch_down:
+        chunk.finish()
+    for chunk in (
+        fetch_query + fetch_key + fetch_value + fetch_out + fetch_gate + fetch_up + fetch_down
+    ):
+        chunk.drain()
+
+
+def attention_forward(tokens_in, out_grad, seg_col, seg_row, freqs, weights):
+    w_query, w_key, w_value, w_out, w_gate, w_up, w_down = weights
+    span = tokens_in.shape[2]
+    length, width = 4 * span, 4 * tokens_in.shape[3]
+    cols = w_query.shape[1] // 2
+    hidden = w_gate.shape[1] // 2
+
+    def low(*shape):
+        return jax.ShapeDtypeStruct(shape, LOW)
+
+    def full(*shape):
+        return jax.ShapeDtypeStruct(shape, FULL)
+
+    in_hbm = [
+        low(width, 3 * cols), low(cols, width), low(width, hidden), low(width, hidden), low(hidden, width),
+        low(length, width), low(length, width), low(length, width),
+    ]
+    in_vmem = [
+        low(length, cols), low(length, cols), low(length, cols), low(length, cols), full(length, cols),
+        full(length, HD), full(length, HD), full(length, HD), full(8, length), full(length // 8, width),
+        full(length // 8, HD), low(length // 8, width),
+    ]
+    vmem = pl.BlockSpec(memory_space=pltpu.VMEM)
+    return pl.pallas_call(
+        attention_kernel,
+        out_shape=in_hbm + in_vmem,
+        in_specs=[HBM] * 4 + [vmem] + [HBM] * 7,
+        out_specs=[HBM] * len(in_hbm) + [vmem] * len(in_vmem),
+        scratch_shapes=[
+            pltpu.VMEM((length, width), LOW),
+            pltpu.VMEM((width, 3 * cols), LOW),
+            pltpu.VMEM((cols, width), LOW),
+            pltpu.VMEM((length // 8, width), LOW),
+            *scatter_buffers(width),
+            pltpu.SemaphoreType.DMA((128,)),
+            pltpu.SemaphoreType.DMA((128,)),
+            pltpu.SemaphoreType.DMA((32,)),
+        ],
+        compiler_params=pltpu.CompilerParams(
+            collective_id=1, has_side_effects=True, vmem_limit_bytes=60 * 1024 * 1024
+        ),
+    )(tokens_in, out_grad, seg_col, seg_row, freqs, *weights)
+
+
 def xor_permute(values, axis, size, mask):
     return lax.ppermute(values, axis, [(place, place ^ mask) for place in range(size)])
 
@@ -353,22 +879,12 @@
     routes = []
     for high in range(2):
         for low in range(2):
-            for model in range(4):
-                wanted = model ^ offset
-                routes.append(
-                    ((high * 2 + low) * 4 + model, ((wanted // 2) * 2 + high) * 4 + low * 2 + wanted % 2)
-                )
+            for chip in range(2):
+                for core in range(2):
+                    source = (high * 2 + low) * 4 + chip * 2 + core
+                    target = (core * 2 + chip) * 4 + ((2 * high + low) ^ offset)
+                    routes.append((source, target))
     return routes
-
-
-def to_rows(values, model_index, quarter):
-    span_half = values.shape[2] // 2
-    parts = values.reshape(4, span_half, values.shape[3])
-    blocks = []
-    for offset in range(4):
-        part = lax.dynamic_index_in_dim(parts, model_index ^ offset, 0, keepdims=False)
-        blocks.append(lax.ppermute(part, ("ctx", "mp"), token_routes(offset)))
-    return jnp.concatenate(pick_blocks(blocks, quarter), axis=1)
 
 
 def from_rows(rows, model_index, quarter):
@@ -377,8 +893,7 @@
     blocks = []
     for offset in range(4):
         part = lax.dynamic_index_in_dim(parts, quarter ^ offset, 0, keepdims=False)
-        routes = [(target, source) for source, target in token_routes(offset)]
-        blocks.append(lax.ppermute(part, ("ctx", "mp"), routes))
+        blocks.append(lax.ppermute(part, ("ctx", "mp"), token_routes(offset)))
     return jnp.concatenate(pick_blocks(blocks, model_index), axis=0).reshape(
         2, 1, 2 * row_count, width // 4
     )
@@ -387,19 +902,6 @@
 def half_of(values, axis, which):
     size = values.shape[axis] // 2
     return lax.dynamic_slice_in_dim(values, which * size, size, axis)
-
-
-def fetch_stack(shards, axis, low, home):
-    mine = jnp.concatenate([half_of(shard, axis, low) for shard in shards], axis=axis)
-    other = jnp.concatenate([half_of(shard, axis, 1 - low) for shard in shards], axis=axis)
-    near = [
-        mine,
-        xor_permute(other, "ctx", 4, 1),
-        xor_permute(mine, "ctx", 4, 2),
-        xor_permute(other, "ctx", 4, 3),
-    ]
-    far = [xor_permute(block, "dp", 2, 1) for block in near]
-    return jnp.concatenate(pick_blocks(near + far, home), axis=1 - axis)
 
 
 def return_grads(grad, axis, dp_index, high, low):
@@ -419,7 +921,10 @@
     return jnp.concatenate([first, second], axis=axis)
 
 
-GROUPS = [[(high * 2 + low) * 4 + model for low in range(2) for model in range(4)] for high in range(2)]
+GROUPS = [
+    [(high * 2 + low) * 4 + chip * 2 + core for core in range(2) for chip in range(2) for low in range(2)]
+    for high in range(2)
+]
 
 
 def gather_rows(rows):
@@ -444,67 +949,52 @@
     model_index = lax.axis_index("mp")
     high = ctx_index // 2
     low = ctx_index % 2
-    quarter = 2 * high + model_index % 2
-    home = dp_index * 4 + ctx_index
+    quarter = 2 * high + low
     score_scale = 1.0 / math.sqrt(HD)
-    feature_width = tokens_in.shape[3] * 4
-
-    segments_all = lax.all_gather(segment_ids, "ctx", axis=2, tiled=True)
-    segment = lax.dynamic_index_in_dim(segments_all, high, 0, keepdims=False)[0]
-    length = segment.shape[0]
+    span = segment_ids.shape[2]
+
+    segment_float = segment_ids[:, 0].astype(jnp.float32)
+    segment_cols = jnp.broadcast_to(segment_float[:, :, None], (2, span, HD))
+    segment_rows = jnp.broadcast_to(segment_float[:, None, :], (2, 8, span))
+    freq_half = jnp.power(10000.0, -2.0 * jnp.arange(HD // 2, dtype=jnp.float32) / HD)
+    freqs = jnp.broadcast_to(jnp.concatenate([freq_half, freq_half])[None], (8, HD))
+    (
+        query_key_value, out_part, gate_part, up_part, down_part, grad_low, second_low, normed_low,
+        query_low, key_low, value_low, mixed_low, log_totals, cosine, sine_part, seg_col, seg_row, residual,
+        inverse_wide, kept,
+    ) = attention_forward(
+        tokens_in, out_grad, segment_cols, segment_rows, freqs,
+        (w_query, w_key, w_value, w_out, w_gate, w_up, w_down),
+    )
+    inverse_two = inverse_wide[:, :1]
+    length = seg_col.shape[0]
     row_count = length // 8
-
-    token_rows = to_rows(tokens_in, model_index, quarter).astype(jnp.float32)
-    query_key_value = fetch_stack((w_query, w_key, w_value), 1, low, home)
-    out_part = fetch_stack((w_out,), 0, low, home)
-    grad_rows = to_rows(out_grad, model_index, quarter)
-    gate_part = fetch_stack((w_gate,), 1, low, home)
-    up_part = fetch_stack((w_up,), 1, low, home)
-    down_part = fetch_stack((w_down,), 0, low, home)
-
-    normed_rows, inverse_one = layer_norm(token_rows)
-    normed_low = gather_rows(normed_rows.astype(jnp.bfloat16))
-
+    local_cols = query_low.shape[1]
+    head_count = local_cols // HD
+    row_start = ((model_index % 2) * 4 + (model_index // 2) * 2 + low) * row_count
+
+    def own_rows(values):
+        return lax.dynamic_slice_in_dim(values, row_start, row_count, 0)
+
+    normed_rows, inverse_one = layer_norm(kept.astype(jnp.float32))
+    grad_rows = own_rows(grad_low)
+    centred = residual - jnp.mean(residual, axis=-1, keepdims=True)
+    normed_two = centred * inverse_two
     places = jnp.arange(length, dtype=jnp.int32)
-    allowed = (segment[:, None] == segment[None, :]) & (places[None, :] <= places[:, None])
-    cosine, sine_part = rope_angles(doc_positions(segment))
-    cosine = cosine[:, None, :]
-    sine_part = sine_part[:, None, :]
-
-    local_cols = query_key_value.shape[1] // 3
-    head_count = local_cols // HD
-    projected = jnp.dot(normed_low, query_key_value, preferred_element_type=jnp.float32)
+    allowed = (seg_col[:, :1] == seg_row[:1]) & (places[None, :] <= places[:, None])
 
     def turned(values, sine_used):
+        parts = values.reshape(length, head_count, 2, HD // 2)
+        swapped = jnp.concatenate([parts[:, :, 1:], parts[:, :, :1]], axis=2)
         return (
-            rope_turn(values.reshape(length, head_count, HD), cosine, sine_used)
+            (
+                parts * cosine.reshape(length, 1, 2, HD // 2)
+                + swapped * sine_used.reshape(length, 1, 2, HD // 2)
+            )
             .astype(jnp.bfloat16)
             .reshape(length, local_cols)
         )
 
-    query_low = turned(projected[:, :local_cols], sine_part)
-    key_low = turned(projected[:, local_cols : 2 * local_cols], sine_part)
-    value_low = projected[:, 2 * local_cols :].astype(jnp.bfloat16)
-    mixed_parts = []
-    log_totals = []
-    for head_index in range(head_count):
-        cols = slice(head_index * HD, (head_index + 1) * HD)
-        scores = dot_rows(query_low[:, cols], key_low[:, cols]) * score_scale
-        scores = jnp.where(allowed, scores, NEG_FILL)
-        highest = jnp.max(scores, axis=-1, keepdims=True)
-        exp_terms = jnp.exp(scores - highest)
-        total_exp = jnp.sum(exp_terms, axis=-1, keepdims=True)
-        probs_low = (exp_terms / total_exp).astype(jnp.bfloat16)
-        mixed_parts.append(
-            jnp.dot(probs_low, value_low[:, cols], preferred_element_type=jnp.float32)
-        )
-        log_totals.append(highest + jnp.log(total_exp))
-    mixed_low = jnp.concatenate(mixed_parts, axis=-1).astype(jnp.bfloat16)
-    branch = scatter_rows(jnp.dot(mixed_low, out_part, preferred_element_type=jnp.float32))
-    residual = token_rows + branch
-    normed_two, inverse_two = layer_norm(residual)
-    second_low = gather_rows(normed_two.astype(jnp.bfloat16))
-    grad_low = gather_rows(grad_rows)
     gate_lin = jnp.dot(second_low, gate_part, preferred_element_type=jnp.float32)
     up_lin = jnp.dot(second_low, up_part, preferred_element_type=jnp.float32)
     sigmoid_gate = jax.nn.sigmoid(gate_lin)
@@ -536,7 +1026,7 @@
         mixed_head = mixed_grad[:, cols]
         scores = dot_rows(query_head, key_head) * score_scale
         scores = jnp.where(allowed, scores, NEG_FILL)
-        probs = jnp.exp(scores - log_totals[head_index])
+        probs = jnp.exp(scores - log_totals[:, head_index * HD : head_index * HD + 1])
         value_parts.append(dot_cols(probs.astype(jnp.bfloat16), mixed_head))
         probs_grad = dot_rows(mixed_head, value_low[:, cols])
         row_dot = jnp.sum(probs * probs_grad, axis=-1, keepdims=True)

time: 986 us -> 912 us (0.925)
  Pallas kernels: 0 us -> 290 us
  waiting for transfers between devices: 581 us -> 366 us
  starting transfers between devices: 99.8 us -> 36.2 us
  blocking collectives: 34.3 us -> 0 us
  local copies, waits for them, and re-layouts: 75.5 us -> 45.1 us
  other arithmetic: 55.6 us -> 45.5 us
    pallas_call x0 -> x1, Pallas kernels: none -> 290 us  [attention_forward(): pl.pallas_call(attention_kernel, out_shape=in_hbm + in_vmem, in_specs=[HB...]
    ppermute x50 -> x15, waiting for transfers between devices: 438 us -> 203 us  [xor_permute(): lax.ppermute(values, axis, [(place, place ^ mask) for place in range(size)])]
    ppermute x50 -> x15, starting transfers between devices: 72.4 us -> 25.9 us  [xor_permute(): lax.ppermute(values, axis, [(place, place ^ mask) for place in range(size)])]
    all_gather x1 -> x0, blocking collectives: 34.3 us -> none  [per_device_grouped(): segments_all = lax.all_gather(segment_ids, 'ctx', axis=2, tiled=True)]
    unnamed x224 -> x95, local copies, waits for them, and re-layouts: 54.9 us -> 27.2 us
    reduce_scatter x4 -> x3, waiting for transfers between devices: 137 us -> 154 us  [scatter_rows(): lax.psum_scatter(terms.astype(jnp.bfloat16), ('ctx', 'mp'), scatter_dimen...]
    ppermute x16 -> x8, starting transfers between devices: 27 us -> 10.2 us  [from_rows(): blocks.append(lax.ppermute(part, ('ctx', 'mp'), token_routes(offset)))]
    dot_general x4 -> x0, matrix products: 11.3 us -> none  [the longest x1 6.22 us: per_device_grouped(): jnp.dot(normed_low, query_key_value, preferred_element_type=jnp.float32)]
  transfers between devices with their start and end apart: 74 -> 27, of which waited for: 33 -> 16; matrix products, arithmetic and copies ran while one was open for 17% -> 14% of each run, Pallas kernels for 0% -> 0%
where the time goes in v2:
time: 912 us; the launch traced here: 900 us
  waiting for transfers between devices  366 us (40%)
  Pallas kernels  290 us (32%)
  matrix products  101 us (11%)
  other arithmetic  45.5 us (5%)
  local copies, waits for them, and re-layouts  45.1 us (5%)
  starting transfers between devices  36.2 us (4%)
  between operations  15.1 us (2%)
    pallas_call x1, Pallas kernels, attention_forward(): pl.pallas_call(attention_kernel, out_shape=in_hbm + in_vmem, in_specs=[HB...  290 us
    ppermute x15, waiting for transfers between devices, xor_permute(): lax.ppermute(values, axis, [(place, place ^ mask) for place in range(size)])  203 us
    reduce_scatter x3, waiting for transfers between devices, scatter_rows(): lax.psum_scatter(terms.astype(jnp.bfloat16), ('ctx', 'mp'), scatter_dimen...  154 us
    dot_general x9, matrix products, dot_rows(): lax.dot_general(left_mat, right_mat, (((1,), (1,)), ((), ())), preferred_...  38.1 us
    unnamed x95, local copies, waits for them, and re-layouts  27.2 us
    ppermute x15, starting transfers between devices, xor_permute(): lax.ppermute(values, axis, [(place, place ^ mask) for place in range(size)])  25.9 us
    dot_general x9, matrix products, dot_cols(): lax.dot_general(left_mat, right_mat, (((0,), (0,)), ((), ())), preferred_...  25.5 us
    dot_general x1, matrix products, per_device_grouped(): jnp.dot(hidden_low, down_part, preferred_element_type=jnp.float32)  20.2 us
  transfers between devices with their start and end apart: 27, of which 16 were waited for; matrix products, arithmetic and copies ran while one was open for 14% of the time, Pallas kernels for 0%

profile of v2, /device:TPU:0, one launch (start us, length us, event | category | flops | bytes accessed | tf_op | source)
XLA Modules:
  0.0 899.8 jit_solution(1660784997484086232)
XLA Ops:
  10.0 290.4 %shard_map.169 = (bf16[2048,768]{1,0:T(8,128)(2,1)}, bf16[256,2048]{1,0:T(8,128)(2,1)}, bf16[2048,1024]{1,0:T(8,128)(2,1)}, bf16[2048,1024]{1,0:T(8,128)(2,1)}, ...) custom-call(bf16[2,1,256,512]{3,2,1,0:T(8,128)(2,1)} %tokens_in.1, ...), custom_call_target="tpu_custom_call" | custom-call | tf_op jit(solution)/shard_map/pallas_call | solution.py:845
  300.4 10.1 %fusion.51 = f32[1024,1024]{1,0:T(8,128)} fusion(bf16[1024,2048]{1,0:T(8,128)(2,1)} %get-tuple-element.30, bf16[2048,1024]{1,0:T(8,128)(2,1)} %get-tuple-element.31), kind=kOutput, calls=%fused_computation.170 | convolution fusion | flops 4294967296 | bytes 12582912 | tf_op jit(solution)/shard_map/dot_general | solution.py:998
  310.5 6.1 fusion.52
  316.7 10.1 %multiply_convert_fusion.2 = (bf16[1024,1024]{1,0:T(8,128)(2,1)}, bf16[1024,1024]{1,0:T(8,128)(2,1)}, bf16[1024,1024]{1,0:T(8,128)(2,1)S(1)}) fusion(f32[1024,1024]{1,0:T(8,128)} %fusion.51, f32[1024,1024]{1,0:T(8,128)} %fusion.52, bf16[1024,2048]{1,0:T(8,128)(2,1)S(1)} %copy-done.26, bf16[1024,2048]{1,0:T(8,128)(2,1)S(1)} %copy-done.32), kind=kOutput, calls=%fused_computation.14 | convolution fusion | flops 4311744512 | bytes 23068672 | tf_op jit(solution)/shard_map/dot_general | solution.py:54
  326.7 6.9 fusion.53
  333.7 7.8 add_convert_fusion
  341.5 20.2 %convolution_convert_fusion.1 = bf16[1024,2048]{1,0:T(8,128)(2,1)} fusion(bf16[1024,1024]{1,0:T(8,128)(2,1)S(1)} %get-tuple-element.77, bf16[1024,2048]{1,0:T(8,128)(2,1)} %get-tuple-element.33), kind=kOutput, calls=%fused_computation.20 | convolution fusion | flops 4297064448 | bytes 10485760 | tf_op jit(solution)/shard_map/dot_general | solution.py:1011
  363.2 65.8 %reduce-scatter.6.cloned.1.call-done = bf16[128,2048]{1,0:T(8,128)(2,1)} async-done(((bf16[1024,2048]{1,0:T(8,128)(2,1)}), bf16[128,2048]{1,0:T(8,128)(2,1)}) %reduce-scatter.6.cloned.1.call-update) | async-done | bytes 524304 | tf_op jit(solution)/shard_map/reduce_scatter | solution.py:935
  430.4 88.6 %reduce-scatter.4.cloned.1.call-done = bf16[128,2048]{1,0:T(8,128)(2,1)} async-done(((bf16[1024,2048]{1,0:T(8,128)(2,1)}), bf16[128,2048]{1,0:T(8,128)(2,1)}) %reduce-scatter.4.cloned.1.call-update) | async-done | bytes 524304 | tf_op jit(solution)/shard_map/reduce_scatter | solution.py:935
  522.3 7.2 fusion.57
  536.0 4.9 fusion.56
  560.6 22.7 %collective-permute-done.20 = bf16[1024,1024]{1,0:T(8,128)(2,1)} collective-permute-done((bf16[1024,1024]{1,0:T(8,128)(2,1)}, bf16[1024,1024]{1,0:T(8,128)(2,1)}, u32[]{:S(2)}, u32[]{:S(2)}) %collective-permute-start.20) | collective-permute-done | bytes 2097184 | tf_op jit(solution)/shard_map/ppermute | solution.py:867
  609.2 5.3 convolution_convert_fusion
  614.5 13.8 %collective-permute-done.17 = bf16[1024,1024]{0,1:T(8,128)(2,1)} collective-permute-done((bf16[1024,1024]{0,1:T(8,128)(2,1)}, bf16[1024,1024]{0,1:T(8,128)(2,1)}, u32[]{:S(2)}, u32[]{:S(2)}) %collective-permute-start.17) | collective-permute-done | bytes 2097184 | tf_op jit(solution)/shard_map/ppermute | solution.py:867
  634.4 37.7 %collective-permute-done.14 = bf16[1024,1024]{0,1:T(8,128)(2,1)} collective-permute-done((bf16[1024,1024]{0,1:T(8,128)(2,1)}, bf16[1024,1024]{0,1:T(8,128)(2,1)}, u32[]{:S(2)}, u32[]{:S(2)}) %collective-permute-start.14) | collective-permute-done | bytes 2097184 | tf_op jit(solution)/shard_map/ppermute | solution.py:867
  681.5 8.8 collective-permute-done.18
  690.8 5.8 collective-permute-start.19
  696.6 30.3 %collective-permute-done.15 = bf16[512,1024]{0,1:T(8,128)(2,1)S(1)} collective-permute-done((bf16[512,1024]{0,1:T(8,128)(2,1)S(1)}, bf16[512,1024]{0,1:T(8,128)(2,1)S(1)}, u32[]{:S(2)}, u32[]{:S(2)}) %collective-permute-start.15) | collective-permute-done | bytes 1048608 | tf_op jit(solution)/shard_map/ppermute | solution.py:867
  731.7 20.8 %collective-permute-done.19 = bf16[256,1024]{0,1:T(8,128)(2,1)S(1)} collective-permute-done((bf16[256,1024]{0,1:T(8,128)(2,1)S(1)}, bf16[256,1024]{0,1:T(8,128)(2,1)S(1)}, u32[]{:S(2)}, u32[]{:S(2)}) %collective-permute-start.19) | collective-permute-done | bytes 524320 | tf_op jit(solution)/shard_map/ppermute | solution.py:867
  762.7 11.9 %collective-permute-done.16 = bf16[256,1024]{0,1:T(8,128)(2,1)S(1)} collective-permute-done((bf16[256,1024]{0,1:T(8,128)(2,1)S(1)}, bf16[256,1024]{0,1:T(8,128)(2,1)S(1)}, u32[]{:S(2)}, u32[]{:S(2)}) %collective-permute-start.16) | collective-permute-done | bytes 524320 | tf_op jit(solution)/shard_map/ppermute | solution.py:867
  783.4 19.6 %collective-permute-done.11 = bf16[256,1024]{0,1:T(8,128)(2,1)} collective-permute-done((bf16[256,1024]{0,1:T(8,128)(2,1)}, bf16[256,1024]{0,1:T(8,128)(2,1)}, u32[]{:S(2)}, u32[]{:S(2)}) %collective-permute-start.11) | collective-permute-done | bytes 524320 | tf_op jit(solution)/shard_map/ppermute | solution.py:867
  824.5 15.6 %collective-permute-done.12 = bf16[256,512]{0,1:T(8,128)(2,1)S(1)} collective-permute-done((bf16[256,512]{0,1:T(8,128)(2,1)}, bf16[256,512]{0,1:T(8,128)(2,1)S(1)}, u32[]{:S(2)}, u32[]{:S(2)}) %collective-permute-start.12) | collective-permute-done | bytes 262176 | tf_op jit(solution)/shard_map/ppermute | solution.py:867
  841.4 14.5 %collective-permute-done.9 = bf16[512,768]{0,1:T(8,128)(2,1)} collective-permute-done((bf16[512,768]{0,1:T(8,128)(2,1)}, bf16[512,768]{0,1:T(8,128)(2,1)}, u32[]{:S(2)}, u32[]{:S(2)}) %collective-permute-start.9) | collective-permute-done | bytes 786464 | tf_op jit(solution)/shard_map/ppermute | solution.py:867
  883.4 8.3 collective-permute-done.5
  (235 shorter events, 151.4 us)
Async XLA Ops:
  7.2 421.8 %reduce-scatter.6.cloned.1.call-start = ((), (), s32[]{:S(2)}) async-start(), calls=%async_computation.4 | async-start | bytes 4718592 | tf_op jit(solution)/shard_map/reduce_scatter | solution.py:935
  341.4 177.6 %reduce-scatter.4.cloned.1.call-start = ((), (), s32[]{:S(2)}) async-start(), calls=%async_computation.3 | async-start | bytes 4718592 | tf_op jit(solution)/shard_map/reduce_scatter | solution.py:935
  361.8 231.0 %all-gather.2.cloned.1.call-start = ((), (), s32[]{:S(2)}) async-start(), calls=%async_computation.5 | async-start | bytes 4718592 | tf_op jit(solution)/shard_map/all_gather | solution.py:931
  522.2 347.1 %reduce-scatter.8.cloned.1.call-start = ((), (), s32[]{:S(2)}) async-start(), calls=%async_computation.6 | async-start | bytes 4718592 | tf_op jit(solution)/shard_map/reduce_scatter | solution.py:935
  534.5 48.8 %collective-permute-start.20 = (bf16[1024,1024]{1,0:T(8,128)(2,1)}, bf16[1024,1024]{1,0:T(8,128)(2,1)}, u32[]{:S(2)}, u32[]{:S(2)}) collective-permute-start(bf16[1024,1024]{1,0:T(8,128)(2,1)} %dynamic-slice_convert_fusion), channel_id=1, source_target_pairs={{0,16},{16,0},{1,17},{17,1},{2,18},{18,2},{3,19},{19,3},{4,20},{20... | collective-permute-start | bytes 6291464 | tf_op jit(solution)/shard_map/ppermute | solution.py:867
  545.2 83.0 %collective-permute-start.17 = (bf16[1024,1024]{0,1:T(8,128)(2,1)}, bf16[1024,1024]{0,1:T(8,128)(2,1)}, u32[]{:S(2)}, u32[]{:S(2)}) collective-permute-start(bf16[1024,1024]{0,1:T(8,128)(2,1)} %dynamic-slice_convert_fusion.1), channel_id=1, source_target_pairs={{0,16},{16,0},{1,17},{17,1},{2,18},{18,2},{3,19},{19,3},{4,20},{20... | collective-permute-start | bytes 6291464 | tf_op jit(solution)/shard_map/ppermute | solution.py:867
  555.6 116.5 %collective-permute-start.14 = (bf16[1024,1024]{0,1:T(8,128)(2,1)}, bf16[1024,1024]{0,1:T(8,128)(2,1)}, u32[]{:S(2)}, u32[]{:S(2)}) collective-permute-start(bf16[1024,1024]{0,1:T(8,128)(2,1)} %dynamic-slice_convert_fusion.2), channel_id=1, source_target_pairs={{0,16},{16,0},{1,17},{17,1},{2,18},{18,2},{3,19},{19,3},{4,20},{20... | collective-permute-start | bytes 6291464 | tf_op jit(solution)/shard_map/ppermute | solution.py:867
  590.4 87.9 %collective-permute-start.21 = (bf16[1024,512]{1,0:T(8,128)(2,1)}, bf16[1024,512]{1,0:T(8,128)(2,1)}, u32[]{:S(2)}, u32[]{:S(2)}) collective-permute-start(bf16[1024,512]{1,0:T(8,128)(2,1)} %dynamic-slice_convert_fusion.4), channel_id=1, source_target_pairs={{0,8},{4,12},{8,0},{12,4},{1,9},{5,13},{9,1},{13,5},{2,10},{6,14},... | collective-permute-start | bytes 3145736 | tf_op jit(solution)/shard_map/ppermute | solution.py:867
  632.0 58.4 %collective-permute-start.18 = (bf16[512,1024]{0,1:T(8,128)(2,1)S(1)}, bf16[512,1024]{0,1:T(8,128)(2,1)S(1)}, u32[]{:S(2)}, u32[]{:S(2)}) collective-permute-start(bf16[512,1024]{0,1:T(8,128)(2,1)S(1)} %dynamic-slice_convert_fusion.5), channel_id=1, source_target_pairs={{0,8},{4,12},{8,0},{12,4},{1,9},{5,13},{9,1},{13,5},{2,10},{6,14},... | collective-permute-start | bytes 3145736 | tf_op jit(solution)/shard_map/ppermute | solution.py:867
  675.8 51.1 %collective-permute-start.15 = (bf16[512,1024]{0,1:T(8,128)(2,1)S(1)}, bf16[512,1024]{0,1:T(8,128)(2,1)S(1)}, u32[]{:S(2)}, u32[]{:S(2)}) collective-permute-start(bf16[512,1024]{0,1:T(8,128)(2,1)S(1)} %dynamic-slice_convert_fusion.6), channel_id=1, source_target_pairs={{0,8},{4,12},{8,0},{12,4},{1,9},{5,13},{9,1},{13,5},{2,10},{6,14},... | collective-permute-start | bytes 3145736 | tf_op jit(solution)/shard_map/ppermute | solution.py:867
  680.0 50.0 %collective-permute-start.22 = (bf16[1024,256]{1,0:T(8,128)(2,1)S(1)}, bf16[1024,256]{1,0:T(8,128)(2,1)S(1)}, u32[]{:S(2)}, u32[]{:S(2)}) collective-permute-start(bf16[1024,256]{1,0:T(8,128)(2,1)S(1)} %dynamic-slice_convert_fusion.8), channel_id=1, source_target_pairs={{0,4},{4,0},{8,12},{12,8},{1,5},{5,1},{9,13},{13,9},{2,6},{6,2},{1... | collective-permute-start | bytes 1572872 | tf_op jit(solution)/shard_map/ppermute | solution.py:867
  690.8 61.7 %collective-permute-start.19 = (bf16[256,1024]{0,1:T(8,128)(2,1)S(1)}, bf16[256,1024]{0,1:T(8,128)(2,1)S(1)}, u32[]{:S(2)}, u32[]{:S(2)}) collective-permute-start(bf16[256,1024]{0,1:T(8,128)(2,1)S(1)} %dynamic-slice_convert_fusion.9), channel_id=1, source_target_pairs={{0,4},{4,0},{8,12},{12,8},{1,5},{5,1},{9,13},{13,9},{2,6},{6,2},{1... | collective-permute-start | bytes 1572872 | tf_op jit(solution)/shard_map/ppermute | solution.py:867
  727.4 47.3 %collective-permute-start.16 = (bf16[256,1024]{0,1:T(8,128)(2,1)S(1)}, bf16[256,1024]{0,1:T(8,128)(2,1)S(1)}, u32[]{:S(2)}, u32[]{:S(2)}) collective-permute-start(bf16[256,1024]{0,1:T(8,128)(2,1)S(1)} %dynamic-slice_convert_fusion.10), channel_id=1, source_target_pairs={{0,4},{4,0},{8,12},{12,8},{1,5},{5,1},{9,13},{13,9},{2,6},{6,2},{1... | collective-permute-start | bytes 1572872 | tf_op jit(solution)/shard_map/ppermute | solution.py:867
  756.4 50.2 %collective-permute-start.8 = (bf16[1024,768]{0,1:T(8,128)(2,1)S(1)}, bf16[1024,768]{0,1:T(8,128)(2,1)}, u32[]{:S(2)}, u32[]{:S(2)}) collective-permute-start(bf16[1024,768]{0,1:T(8,128)(2,1)S(1)} %dynamic-slice_convert_fusion.3), channel_id=1, source_target_pairs={{0,16},{16,0},{1,17},{17,1},{2,18},{18,2},{3,19},{19,3},{4,20},{20... | collective-permute-start | bytes 4718600 | tf_op jit(solution)/shard_map/ppermute | solution.py:867
  760.6 42.4 %collective-permute-start.11 = (bf16[256,1024]{0,1:T(8,128)(2,1)}, bf16[256,1024]{0,1:T(8,128)(2,1)}, u32[]{:S(2)}, u32[]{:S(2)}) collective-permute-start(bf16[256,1024]{0,1:T(8,128)(2,1)} %dynamic-slice_convert_fusion.11), channel_id=1, source_target_pairs={{0,16},{16,0},{1,17},{17,1},{2,18},{18,2},{3,19},{19,3},{4,20},{20... | collective-permute-start | bytes 1572872 | tf_op jit(solution)/shard_map/ppermute | solution.py:867
  779.1 36.2 %collective-permute-start.3 = (bf16[128,512]{1,0:T(8,128)(2,1)S(1)}, bf16[128,512]{1,0:T(8,128)(2,1)S(1)}, u32[]{:S(2)}, u32[]{:S(2)}) collective-permute-start(bf16[128,512]{1,0:T(8,128)(2,1)S(1)} %bitcast.111), channel_id=1, source_target_pairs={{0,3},{1,11},{2,7},{3,15},{4,2},{5,10},{6,6},{7,14},{8,1},{9,9},{1... | collective-permute-start | bytes 393224 | tf_op jit(solution)/shard_map/ppermute | solution.py:896
  781.6 41.7 %collective-permute-start.1 = (bf16[128,512]{1,0:T(8,128)(2,1)}, bf16[128,512]{1,0:T(8,128)(2,1)}, u32[]{:S(2)}, u32[]{:S(2)}) collective-permute-start(bf16[128,512]{1,0:T(8,128)(2,1)} %bitcast.99), channel_id=1, source_target_pairs={{0,1},{1,9},{2,5},{3,13},{4,0},{5,8},{6,4},{7,12},{8,3},{9,11},{10... | collective-permute-start | bytes 393224 | tf_op jit(solution)/shard_map/ppermute | solution.py:896
  781.6 41.7 %collective-permute-start.2 = (bf16[128,512]{1,0:T(8,128)(2,1)}, bf16[128,512]{1,0:T(8,128)(2,1)}, u32[]{:S(2)}, u32[]{:S(2)}) collective-permute-start(bf16[128,512]{1,0:T(8,128)(2,1)} %bitcast.98), channel_id=1, source_target_pairs={{0,2},{1,10},{2,6},{3,14},{4,3},{5,11},{6,7},{7,15},{8,0},{9,8},{1... | collective-permute-start | bytes 393224 | tf_op jit(solution)/shard_map/ppermute | solution.py:896
  803.0 20.3 %collective-permute-start = (bf16[128,512]{1,0:T(8,128)(2,1)S(1)}, bf16[128,512]{1,0:T(8,128)(2,1)}, u32[]{:S(2)}, u32[]{:S(2)}) collective-permute-start(bf16[128,512]{1,0:T(8,128)(2,1)S(1)} %bitcast.108), channel_id=1, source_target_pairs={{0,0},{1,8},{2,4},{3,12},{4,1},{5,9},{6,5},{7,13},{8,2},{9,10},{10... | collective-permute-start | bytes 393224 | tf_op jit(solution)/shard_map/ppermute | solution.py:896
  806.8 33.4 %collective-permute-start.12 = (bf16[256,512]{0,1:T(8,128)(2,1)}, bf16[256,512]{0,1:T(8,128)(2,1)S(1)}, u32[]{:S(2)}, u32[]{:S(2)}) collective-permute-start(bf16[256,512]{0,1:T(8,128)(2,1)} %dynamic-slice_convert_fusion.13), channel_id=1, source_target_pairs={{0,8},{4,12},{8,0},{12,4},{1,9},{5,13},{9,1},{13,5},{2,10},{6,14},... | collective-permute-start | bytes 786440 | tf_op jit(solution)/shard_map/ppermute | solution.py:867
  815.9 39.9 %collective-permute-start.9 = (bf16[512,768]{0,1:T(8,128)(2,1)}, bf16[512,768]{0,1:T(8,128)(2,1)}, u32[]{:S(2)}, u32[]{:S(2)}) collective-permute-start(bf16[512,768]{0,1:T(8,128)(2,1)} %dynamic-slice_convert_fusion.7), channel_id=1, source_target_pairs={{0,8},{4,12},{8,0},{12,4},{1,9},{5,13},{9,1},{13,5},{2,10},{6,14},... | collective-permute-start | bytes 2359304 | tf_op jit(solution)/shard_map/ppermute | solution.py:867
  841.3 18.0 %collective-permute-start.13 = (bf16[256,256]{0,1:T(8,128)(2,1)S(1)}, bf16[256,256]{0,1:T(8,128)(2,1)S(1)}, u32[]{:S(2)}, u32[]{:S(2)}) collective-permute-start(bf16[256,256]{0,1:T(8,128)(2,1)S(1)} %dynamic-slice_convert_fusion.14), channel_id=1, source_target_pairs={{0,4},{4,0},{8,12},{12,8},{1,5},{5,1},{9,13},{13,9},{2,6},{6,2},{1... | collective-permute-start | bytes 393224 | tf_op jit(solution)/shard_map/ppermute | solution.py:867
  875.8 15.9 %collective-permute-start.5 = (bf16[128,512]{1,0:T(8,128)(2,1)S(1)}, bf16[128,512]{1,0:T(8,128)(2,1)S(1)}, u32[]{:S(2)}, u32[]{:S(2)}) collective-permute-start(bf16[128,512]{1,0:T(8,128)(2,1)S(1)} %bitcast.112), channel_id=1, source_target_pairs={{0,1},{1,9},{2,5},{3,13},{4,0},{5,8},{6,4},{7,12},{8,3},{9,11},{10... | collective-permute-start | bytes 393224 | tf_op jit(solution)/shard_map/ppermute | solution.py:896
  875.9 15.8 %collective-permute-start.6 = (bf16[128,512]{1,0:T(8,128)(2,1)S(1)}, bf16[128,512]{1,0:T(8,128)(2,1)S(1)}, u32[]{:S(2)}, u32[]{:S(2)}) collective-permute-start(bf16[128,512]{1,0:T(8,128)(2,1)S(1)} %bitcast.110), channel_id=1, source_target_pairs={{0,2},{1,10},{2,6},{3,14},{4,3},{5,11},{6,7},{7,15},{8,0},{9,8},{1... | collective-permute-start | bytes 393224 | tf_op jit(solution)/shard_map/ppermute | solution.py:896
  (43 other events, 356.9 us)
Sparse Core Ops, SparseCore 0:
  341.6 87.4 reduce-scatter.5
  431.3 87.6 reduce-scatter.3
  522.3 29.1 all-gather.1
  614.6 193.6 reduce-scatter.7
